TPU v7x, 32 devices: a whole 2x2x4 slice. The times are simulated.
32 devices in a mesh: ctx: 8 (over z, x), ch: 4 (over y, core).
Axes of the slice: x: 2, y: 2, z: 4, core: 2. Of those that a mesh axis runs over, the one named last changes fastest.
Arguments:
- tokens: bfloat16 [1024, 4096], P('ctx'), may hold values from -6 to 6
- value_weight: bfloat16 [4096, 2048], P(None, 'ch'), may hold values from -0.09375 to 0.09375
- gate_rows: bfloat16 [1024, 2048], P('ctx', 'ch'), may hold values from -6 to 6
- filter_taps: bfloat16 [1024, 2048], P('ctx', 'ch'), may hold values from -0.1875 to 0.1875
- out_weight: bfloat16 [2048, 4096], P('ch'), may hold values from -0.1875 to 0.1875
Outputs:
- mixed_out: bfloat16 [1024, 4096], P('ctx', 'ch')
All inputs are finite; a program needn't handle non-finite values.
Results may differ from a plain program's by a relative error of at most 0.0095.
Values may be sent and summed in bfloat16 or wider, within the bound.
No kernel may reach another device: no remote copies, remote signals or barrier semaphores. Data moves between devices by JAX's collectives and lax.ppermute only.
A program may use at most 64 MiB of HBM per device.

v0:
```python
import math

import jax
import jax.numpy as jnp
from jax import lax
from jax.sharding import PartitionSpec as P

HIGHEST = lax.Precision.HIGHEST


def column_tables(half_rows, peer_count):
    rows_full = 2 * half_rows
    length = rows_full * peer_count
    outer_freq = jnp.arange(rows_full, dtype=jnp.int32)[:, None]
    outer_pos = jnp.arange(half_rows, dtype=jnp.int32)[None, :]
    first_angle = (
        -2.0 * math.pi / rows_full * (outer_freq * outer_pos % rows_full).astype(jnp.float32)
    )
    inner_pos = jnp.arange(peer_count, dtype=jnp.int32)[None, :]
    twist_angle = -2.0 * math.pi / length * (outer_freq * inner_pos % length).astype(jnp.float32)
    inner_index = jnp.arange(peer_count, dtype=jnp.int32)
    second_angle = (
        -2.0
        * math.pi
        / peer_count
        * (inner_index[:, None] * inner_index[None, :] % peer_count).astype(jnp.float32)
    )
    return (
        jnp.cos(first_angle),
        jnp.sin(first_angle),
        jnp.cos(twist_angle),
        jnp.sin(twist_angle),
        jnp.cos(second_angle),
        jnp.sin(second_angle),
    )


def column_spectrum(signal, tables):
    first_cos, first_sin, twist_cos, twist_sin, second_cos, second_sin = tables
    section_real = jnp.einsum("kn,nbc->ckb", first_cos, signal, precision=HIGHEST)
    section_imag = jnp.einsum("kn,nbc->ckb", first_sin, signal, precision=HIGHEST)
    turned_real = section_real * twist_cos - section_imag * twist_sin
    turned_imag = section_real * twist_sin + section_imag * twist_cos

    def apply_second(table_part, operand):
        return jnp.einsum("ckb,bj->ckj", operand, table_part, precision=HIGHEST)

    spec_real = apply_second(second_cos, turned_real) - apply_second(second_sin, turned_imag)
    spec_imag = apply_second(second_sin, turned_real) + apply_second(second_cos, turned_imag)
    return (spec_real, spec_imag)


def column_inverse(spec_real, spec_imag, tables):
    first_cos, first_sin, twist_cos, twist_sin, second_cos, second_sin = tables

    def apply_second(table_part, operand):
        return jnp.einsum("ckj,bj->ckb", operand, table_part, precision=HIGHEST)

    back_real = apply_second(second_cos, spec_real) + apply_second(second_sin, spec_imag)
    back_imag = apply_second(second_cos, spec_imag) - apply_second(second_sin, spec_real)
    turned_real = back_real * twist_cos + back_imag * twist_sin
    turned_imag = back_imag * twist_cos - back_real * twist_sin
    return jnp.einsum("kn,ckb->nbc", first_cos, turned_real, precision=HIGHEST) + jnp.einsum(
        "kn,ckb->nbc", first_sin, turned_imag, precision=HIGHEST
    )


def on_device(tokens, value_weight, gate_rows, filter_taps, out_weight):
    local_rows = tokens.shape[0]
    peer_count = lax.axis_size("ctx")
    length = peer_count * local_rows
    value_rows = jnp.dot(tokens, value_weight, preferred_element_type=jnp.float32).astype(
        jnp.bfloat16
    )
    value_columns = lax.all_to_all(value_rows, "ctx", split_axis=1, concat_axis=0, tiled=True)
    tap_columns = lax.all_to_all(filter_taps, "ctx", split_axis=1, concat_axis=0, tiled=True)
    channels_here = value_columns.shape[1]
    tables = column_tables(local_rows, peer_count)
    value_signal = value_columns.astype(jnp.float32).reshape(local_rows, peer_count, channels_here)
    tap_signal = tap_columns.astype(jnp.float32).reshape(local_rows, peer_count, channels_here)
    value_real, value_imag = column_spectrum(value_signal, tables)
    tap_real, tap_imag = column_spectrum(tap_signal, tables)
    product_real = value_real * tap_real - value_imag * tap_imag
    product_imag = value_real * tap_imag + value_imag * tap_real
    restored = column_inverse(product_real, product_imag, tables) / (2.0 * length)
    restored = restored.reshape(length, channels_here).astype(jnp.bfloat16)
    convolved = lax.all_to_all(restored, "ctx", split_axis=0, concat_axis=1, tiled=True)
    gated_rows = (convolved.astype(jnp.float32) * gate_rows.astype(jnp.float32)).astype(
        jnp.bfloat16
    )
    partial_sum = jnp.dot(gated_rows, out_weight, preferred_element_type=jnp.float32)
    own_sum = lax.psum_scatter(
        partial_sum.astype(jnp.bfloat16), "ch", scatter_dimension=1, tiled=True
    )
    return own_sum


def solution(mesh):
    placed = (P("ctx", None), P(None, "ch"), P("ctx", "ch"), P("ctx", "ch"), P("ch", None))
    return jax.shard_map(
        on_device, mesh=mesh, in_specs=placed, out_specs=P("ctx", "ch"), check_vma=False
    )
```

profile of v0, /device:TPU:0, one launch (start us, length us, event | category | flops | bytes accessed | tf_op | source)
XLA Modules:
  0.0 92.6 jit_solution(1263056263399420584)
XLA Ops:
  6.5 1.8 %copy.69 = bf16[128,512]{0,1:T(8,128)(2,1)} copy(bf16[128,512]{1,0:T(8,128)(2,1)} %param.8) | data formatting | bytes 262144 | tf_op args[3]
  8.3 7.3 %all-to-all-start.1 = ((bf16[128,8,64]{0,2,1:T(8,128)(2,1)}), bf16[128,8,64]{0,2,1:T(8,128)(2,1)S(1)}, u32[]{:S(2)}, u32[]{:S(2)}) async-start(bf16[128,8,64]{0,2,1:T(8,128)(2,1)} %bitcast.9), calls=%async_computation.1 | async-start | bytes 262144 | tf_op jit(solution)/shard_map/all_to_all | solution.py:76
  15.5 2.9 %convolution_convert_fusion.1 = bf16[128,512]{1,0:T(8,128)(2,1)S(1)} fusion(bf16[128,4096]{1,0:T(8,128)(2,1)S(1)} %copy-done, bf16[4096,512]{1,0:T(8,128)(2,1)} %param.6), kind=kOutput, calls=%fused_computation.9 | convolution fusion | flops 536936448 | bytes 5373952 | tf_op jit(solution)/shard_map/dot_general | solution.py:72
  18.5 0.8 copy.61
  19.3 3.6 %all-to-all-done.1 = bf16[128,8,64]{0,2,1:T(8,128)(2,1)S(1)} async-done(((bf16[128,8,64]{0,2,1:T(8,128)(2,1)}), bf16[128,8,64]{0,2,1:T(8,128)(2,1)S(1)}, u32[]{:S(2)}, u32[]{:S(2)}) %all-to-all-start.1) | async-done | bytes 131104 | tf_op jit(solution)/shard_map/all_to_all | solution.py:76
  22.9 3.4 %all-to-all-start = ((bf16[128,8,64]{0,2,1:T(8,128)(2,1)}), bf16[128,8,64]{0,2,1:T(8,128)(2,1)S(1)}, u32[]{:S(2)}, u32[]{:S(2)}) async-start(bf16[128,8,64]{0,2,1:T(8,128)(2,1)} %bitcast), calls=%async_computation | async-start | bytes 262144 | tf_op jit(solution)/shard_map/all_to_all | solution.py:75
  26.7 0.9 fusion.36
  27.5 0.9 fusion.32
  28.5 0.9 %fusion.8 = f32[64,256,8]{1,2,0:T(8,128)S(1)} fusion(f32[64,256,8]{1,0,2:T(8,128)S(1)} %get-tuple-element.10), kind=kOutput, calls=%fused_computation.27 | convolution fusion | flops 12583808 | bytes 1048576 | tf_op jit(solution)/shard_map/ckb,bj->ckj/dot_general | solution.py:46
  29.5 0.9 %fusion.10 = f32[64,256,8]{1,2,0:T(8,128)S(1)} fusion(f32[64,256,8]{1,0,2:T(8,128)S(1)} %get-tuple-element.10), kind=kOutput, calls=%fused_computation.29 | convolution fusion | flops 12583808 | bytes 1048576 | tf_op jit(solution)/shard_map/ckb,bj->ckj/dot_general | solution.py:46
  30.4 3.1 %all-to-all-done = bf16[128,8,64]{0,2,1:T(8,128)(2,1)S(1)} async-done(((bf16[128,8,64]{0,2,1:T(8,128)(2,1)}), bf16[128,8,64]{0,2,1:T(8,128)(2,1)S(1)}, u32[]{:S(2)}, u32[]{:S(2)}) %all-to-all-start) | async-done | bytes 131104 | tf_op jit(solution)/shard_map/all_to_all | solution.py:75
  33.9 0.9 convolution_bitcast_fusion.1
  34.8 0.9 multiply_add_fusion.2
  35.7 0.9 %fusion.14 = f32[64,256,8]{1,2,0:T(8,128)S(1)} fusion(f32[64,256,8]{1,0,2:T(8,128)S(1)} %get-tuple-element.12), kind=kOutput, calls=%fused_computation.33 | convolution fusion | flops 12583808 | bytes 1048576 | tf_op jit(solution)/shard_map/ckb,bj->ckj/dot_general | solution.py:46
  36.7 0.9 %fusion.16 = f32[64,256,8]{1,2,0:T(8,128)S(1)} fusion(f32[64,256,8]{1,0,2:T(8,128)S(1)} %get-tuple-element.12), kind=kOutput, calls=%fused_computation.35 | convolution fusion | flops 12583808 | bytes 1048576 | tf_op jit(solution)/shard_map/ckb,bj->ckj/dot_general | solution.py:46
  37.6 0.9 %convolution_subtract_fusion = f32[64,256,8]{1,2,0:T(8,128)S(1)} fusion(f32[64,256,8]{1,2,0:T(8,128)S(1)} %fusion.10, f32[64,256,8]{1,0,2:T(8,128)S(1)} %get-tuple-element.9), kind=kOutput, calls=%fused_computation.5 | convolution fusion | flops 12714880 | bytes 1572864 | tf_op jit(solution)/shard_map/ckb,bj->ckj/dot_general | solution.py:46
  38.5 0.9 %convolution_add_fusion = f32[64,256,8]{1,2,0:T(8,128)S(1)} fusion(f32[64,256,8]{1,2,0:T(8,128)S(1)} %fusion.8, f32[64,256,8]{1,0,2:T(8,128)S(1)} %get-tuple-element.9), kind=kOutput, calls=%fused_computation.3 | convolution fusion | flops 12714880 | bytes 1572864 | tf_op jit(solution)/shard_map/ckb,bj->ckj/dot_general | solution.py:46
  39.5 0.9 %convolution_subtract_fusion.1 = f32[64,256,8]{1,2,0:T(8,128)S(1)} fusion(f32[64,256,8]{1,2,0:T(8,128)S(1)} %fusion.16, f32[64,256,8]{1,0,2:T(8,128)S(1)} %get-tuple-element.11), kind=kOutput, calls=%fused_computation.6 | convolution fusion | flops 12714880 | bytes 1572864 | tf_op jit(solution)/shard_map/ckb,bj->ckj/dot_general | solution.py:46
  40.4 1.1 %multiply_subtract_fusion.1 = (f32[64,256,8]{1,2,0:T(8,128)S(1)}, f32[64,256,8]{1,2,0:T(8,128)S(1)}) fusion(f32[64,256,8]{1,2,0:T(8,128)S(1)} %convolution_add_fusion, f32[64,256,8]{1,2,0:T(8,128)S(1)} %convolution_subtract_fusion.1, f32[64,256,8]{1,2,0:T(8,128)S(1)} %convolution_subtract_fusion, f32[64,256,8]{1,2,0:T(8,128)S(1)} %fusion.14, ...), kind=kOutput, calls=%fused_computation.20 | convolution fusion | flops 13501312 | bytes 3670016 | tf_op jit(solution)/shard_map/ckb,bj->ckj/dot_general | solution.py:46
  41.5 0.8 fusion.48
  42.2 0.6 fusion.58
  42.9 0.6 fusion.56
  43.5 0.6 fusion.50
  44.1 0.6 multiply_subtract_fusion
  44.7 1.3 %fusion.4 = f32[64,8,128]{2,1,0:T(8,128)S(1)} fusion(f32[64,256,8]{1,0,2:T(8,128)S(1)} %get-tuple-element.6), kind=kOutput, calls=%fused_computation.13 | convolution fusion | flops 201785344 | bytes 786432 | tf_op jit(solution)/shard_map/kn,ckb->nbc/dot_general | solution.py:63
  46.0 1.3 %fusion.2 = bf16[128,8,64]{0,1,2:T(8,128)(2,1)S(1)} fusion(f32[64,8,128]{2,1,0:T(8,128)S(1)} %fusion.4, f32[64,256,8]{1,0,2:T(8,128)S(1)} %get-tuple-element.5), kind=kOutput, calls=%fused_computation.11 | convolution fusion | flops 201981952 | bytes 917504 | tf_op jit(solution)/shard_map/kn,ckb->nbc/dot_general | solution.py:63
  47.3 0.2 copy.91
  47.5 0.8 copy.92
  48.3 3.4 %all-to-all-start.2 = ((bf16[8,128,64]{1,2,0:T(8,128)(2,1)}), bf16[8,128,64]{1,2,0:T(8,128)(2,1)S(1)}, u32[]{:S(2)}, u32[]{:S(2)}) async-start(bf16[8,128,64]{1,2,0:T(8,128)(2,1)} %copy.92), calls=%async_computation.2 | async-start | bytes 262144 | tf_op jit(solution)/shard_map/all_to_all | solution.py:87
  51.8 7.1 %all-to-all-done.2 = bf16[8,128,64]{1,2,0:T(8,128)(2,1)S(1)} async-done(((bf16[8,128,64]{1,2,0:T(8,128)(2,1)}), bf16[8,128,64]{1,2,0:T(8,128)(2,1)S(1)}, u32[]{:S(2)}, u32[]{:S(2)}) %all-to-all-start.2) | async-done | bytes 131104 | tf_op jit(solution)/shard_map/all_to_all | solution.py:87
  59.0 3.9 %convolution_convert_fusion = bf16[128,4096]{1,0:T(8,128)(2,1)} fusion(bf16[128,512]{0,1:T(8,128)(2,1)S(1)} %fusion.18, bf16[512,4096]{1,0:T(8,128)(2,1)} %param.9), kind=kOutput, calls=%fused_computation | convolution fusion | flops 537395200 | bytes 5373952 | tf_op jit(solution)/shard_map/dot_general | solution.py:91
  62.9 22.8 %reduce-scatter.2.cloned.1.call-done = bf16[128,1024]{1,0:T(8,128)(2,1)} async-done(((bf16[128,4096]{1,0:T(8,128)(2,1)}), bf16[128,1024]{1,0:T(8,128)(2,1)}) %reduce-scatter.2.cloned.1.call-update) | async-done | bytes 262160 | tf_op jit(solution)/shard_map/reduce_scatter | solution.py:92
  (14 shorter events, 1.2 us)
Async XLA Ops:
  6.5 9.0 %copy-start = (bf16[128,4096]{1,0:T(8,128)(2,1)S(1)}, bf16[128,4096]{1,0:T(8,128)(2,1)}, u32[]{:S(2)}) copy-start(bf16[128,4096]{1,0:T(8,128)(2,1)} %param.5) | copy-start | bytes 3145732
  8.3 14.6 %all-to-all-start.1 = ((bf16[128,8,64]{0,2,1:T(8,128)(2,1)}), bf16[128,8,64]{0,2,1:T(8,128)(2,1)S(1)}, u32[]{:S(2)}, u32[]{:S(2)}) async-start(bf16[128,8,64]{0,2,1:T(8,128)(2,1)} %bitcast.9), calls=%async_computation.1 | async-start | bytes 262144 | tf_op jit(solution)/shard_map/all_to_all | solution.py:76
  22.9 10.7 %all-to-all-start = ((bf16[128,8,64]{0,2,1:T(8,128)(2,1)}), bf16[128,8,64]{0,2,1:T(8,128)(2,1)S(1)}, u32[]{:S(2)}, u32[]{:S(2)}) async-start(bf16[128,8,64]{0,2,1:T(8,128)(2,1)} %bitcast), calls=%async_computation | async-start | bytes 262144 | tf_op jit(solution)/shard_map/all_to_all | solution.py:75
  42.8 8.9 %copy-start.1 = (bf16[128,512]{1,0:T(8,128)(2,1)S(1)}, bf16[128,512]{1,0:T(8,128)(2,1)}, u32[]{:S(2)}) copy-start(bf16[128,512]{1,0:T(8,128)(2,1)} %param.7) | copy-start | bytes 393220
  48.3 10.7 %all-to-all-start.2 = ((bf16[8,128,64]{1,2,0:T(8,128)(2,1)}), bf16[8,128,64]{1,2,0:T(8,128)(2,1)S(1)}, u32[]{:S(2)}, u32[]{:S(2)}) async-start(bf16[8,128,64]{1,2,0:T(8,128)(2,1)} %copy.92), calls=%async_computation.2 | async-start | bytes 262144 | tf_op jit(solution)/shard_map/all_to_all | solution.py:87
  51.7 34.1 %reduce-scatter.2.cloned.1.call-start = ((), (), s32[]{:S(2)}) async-start(), calls=%async_computation.4 | async-start | bytes 1310720 | tf_op jit(solution)/shard_map/reduce_scatter | solution.py:92
Sparse Core Ops, SparseCore 0:
  63.0 22.6 reduce-scatter.1
where the time goes:
time: 93.1 us; the launch traced here: 92.6 us
  waiting for transfers between devices  36.7 us (39%)
  matrix products  23 us (25%)
  starting transfers between devices  14 us (15%)
  between operations  13.6 us (15%)
  local copies, waits for them, and re-layouts  4.39 us (5%)
    reduce_scatter x1, waiting for transfers between devices, on_device(): lax.psum_scatter(partial_sum.astype(jnp.bfloat16), 'ch', scatter_dimensio...  22.8 us
    dot_general x8, matrix products, apply_second(): return jnp.einsum('ckb,bj->ckj', operand, table_part, precision=HIGHEST)  7.55 us
    all_to_all x1, starting transfers between devices, on_device(): lax.all_to_all(filter_taps, 'ctx', split_axis=1, concat_axis=0, tiled=True)  7.25 us
    all_to_all x1, waiting for transfers between devices, on_device(): lax.all_to_all(restored, 'ctx', split_axis=0, concat_axis=1, tiled=True)  7.1 us
    dot_general x1, matrix products, on_device(): jnp.dot(gated_rows, out_weight, preferred_element_type=jnp.float32)  3.91 us
    all_to_all x1, waiting for transfers between devices, on_device(): lax.all_to_all(filter_taps, 'ctx', split_axis=1, concat_axis=0, tiled=True)  3.6 us
    all_to_all x1, starting transfers between devices, on_device(): lax.all_to_all(restored, 'ctx', split_axis=0, concat_axis=1, tiled=True)  3.37 us
    all_to_all x1, starting transfers between devices, on_device(): lax.all_to_all(value_rows, 'ctx', split_axis=1, concat_axis=0, tiled=True)  3.37 us
  transfers between devices with their start and end apart: 4, of which 4 were waited for; matrix products, arithmetic and copies ran while one was open for 9% of the time, Pallas kernels for 0%

commit v1 on v0

--- a/solution.py
+++ b/solution.py
@@ -2,7 +2,10 @@
 
 import jax
 import jax.numpy as jnp
+import numpy as np
 from jax import lax
+from jax.experimental import pallas as pl
+from jax.experimental.pallas import tpu as pltpu
 from jax.sharding import PartitionSpec as P
 
 HIGHEST = lax.Precision.HIGHEST
@@ -65,7 +68,7 @@
     )
 
 
-def on_device(tokens, value_weight, gate_rows, filter_taps, out_weight):
+def by_transform(tokens, value_weight, gate_rows, filter_taps, out_weight):
     local_rows = tokens.shape[0]
     peer_count = lax.axis_size("ctx")
     length = peer_count * local_rows
@@ -95,6 +98,249 @@
     return own_sum
 
 
+LANES = 128
+SHIFTS = 16
+GROUP = 16
+NT = (((1,), (1,)), ((), ()))
+TN = (((0,), (0,)), ((), ()))
+
+
+def value_kernel(tokens_ref, weight_ref, taps_ref, gate_ref, payload_ref, gate_t_ref, total_ref):
+    step = pl.program_id(0)
+    peers, both, rows = payload_ref.shape
+    part = both // 2
+
+    @pl.when(step == 0)
+    def _():
+        total_ref[...] = jnp.zeros_like(total_ref)
+        row = lax.broadcasted_iota(jnp.int32, (rows, rows), 0)
+        column = lax.broadcasted_iota(jnp.int32, (rows, rows), 1)
+        flip = jnp.where(row + column == rows - 1, 1.0, 0.0).astype(jnp.bfloat16)
+        flipped = jnp.dot(flip, taps_ref[...], preferred_element_type=jnp.float32)
+        flipped_t = flipped.T.astype(jnp.bfloat16)
+        for peer in range(peers):
+            payload_ref[peer, part:, :] = flipped_t[peer * part : (peer + 1) * part]
+        gate_t_ref[...] = gate_ref[...].astype(jnp.float32).T.astype(jnp.bfloat16)
+
+    total_ref[...] += jnp.dot(
+        tokens_ref[...], weight_ref[...], preferred_element_type=jnp.float32
+    )
+
+    @pl.when(step == pl.num_programs(0) - 1)
+    def _():
+        value_t = total_ref[...].T.astype(jnp.bfloat16)
+        for peer in range(peers):
+            payload_ref[peer, :part, :] = value_t[peer * part : (peer + 1) * part]
+
+
+def value_payload(tokens, value_weight, filter_taps, gate_rows, peers):
+    rows, depth = tokens.shape
+    channels = value_weight.shape[1]
+    steps = 4
+    block = depth // steps
+    return pl.pallas_call(
+        value_kernel,
+        grid=(steps,),
+        in_specs=[
+            pl.BlockSpec((rows, block), lambda k: (0, k)),
+            pl.BlockSpec((block, channels), lambda k: (k, 0)),
+            pl.BlockSpec((rows, channels), lambda k: (0, 0)),
+            pl.BlockSpec((rows, channels), lambda k: (0, 0)),
+        ],
+        out_specs=[
+            pl.BlockSpec((peers, 2 * channels // peers, rows), lambda k: (0, 0, 0)),
+            pl.BlockSpec((channels, rows), lambda k: (0, 0)),
+        ],
+        out_shape=[
+            jax.ShapeDtypeStruct((peers, 2 * channels // peers, rows), jnp.bfloat16),
+            jax.ShapeDtypeStruct((channels, rows), jnp.bfloat16),
+        ],
+        scratch_shapes=[pltpu.VMEM((rows, channels), jnp.float32)],
+        compiler_params=pltpu.CompilerParams(vmem_limit_bytes=16 * 2**20),
+    )(tokens, value_weight, filter_taps, gate_rows)
+
+
+def conv_kernel(payload_ref, place_ref, out_ref, value_ref, taps_ref, picked_ref):
+    blocks, both, lanes = payload_ref.shape
+    channels = both // 2
+    length = blocks * lanes
+    outer = lanes // SHIFTS
+    tail = jnp.zeros((GROUP, lanes), jnp.float32)
+    rows = 2 * outer * GROUP
+    row = lax.broadcasted_iota(jnp.int32, (rows, SHIFTS * GROUP), 0)
+    column = lax.broadcasted_iota(jnp.int32, (rows, SHIFTS * GROUP), 1)
+    same = row % GROUP == column % GROUP
+    for group in range(channels // GROUP):
+        first = group * GROUP
+        padded = jnp.concatenate(
+            [
+                payload_ref[q, first : first + GROUP, :].astype(jnp.float32)
+                for q in range(blocks)
+            ]
+            + [tail],
+            axis=1,
+        )
+        for shift in range(SHIFTS):
+            moved = pltpu.roll(padded, shift, 1) if shift else padded
+            value_ref[group, shift * GROUP : (shift + 1) * GROUP, :] = moved[:, :length].astype(
+                jnp.bfloat16
+            )
+        padded = jnp.concatenate(
+            [
+                payload_ref[blocks - 1 - q, channels + first : channels + first + GROUP, :].astype(
+                    jnp.float32
+                )
+                for q in range(blocks)
+            ]
+            + [tail],
+            axis=1,
+        )
+        for k in range(outer):
+            left = SHIFTS * (outer - 1 - k)
+            moved = pltpu.roll(padded, length + lanes - left, 1) if left else padded
+            taps_ref[group, k * GROUP : (k + 1) * GROUP, :length] = moved[:, :length].astype(
+                jnp.bfloat16
+            )
+        taps_ref[group, :, length:] = jnp.zeros((outer * GROUP, lanes), jnp.bfloat16)
+        for pair in range(blocks // 2):
+            depth = 2 * lanes * (pair + 1)
+            even = (blocks - 1 - 2 * pair) * lanes
+            odd = even - lanes
+            left_side = jnp.concatenate(
+                [
+                    taps_ref[group, :, even : even + depth],
+                    taps_ref[group, :, odd : odd + depth],
+                ],
+                axis=0,
+            )
+            mixed = lax.dot_general(
+                left_side, value_ref[group, :, :depth], NT, preferred_element_type=jnp.float32
+            )
+            picked = jnp.where(same, mixed, 0.0).astype(jnp.bfloat16)
+            for half in range(2):
+                block = 2 * pair + half
+                for k in range(outer):
+                    at = (half * outer + k) * GROUP
+                    picked_ref[
+                        group,
+                        block * GROUP : (block + 1) * GROUP,
+                        k * SHIFTS * GROUP : (k + 1) * SHIFTS * GROUP,
+                    ] = picked[at : at + GROUP]
+        result = jnp.dot(picked_ref[group], place_ref[...], preferred_element_type=jnp.float32)
+        result = result.astype(jnp.bfloat16)
+        for block in range(blocks):
+            out_ref[block, first : first + GROUP, :] = result[block * GROUP : (block + 1) * GROUP]
+
+
+def placement(lanes):
+    outer = lanes // SHIFTS
+    k, r, _, t = np.ix_(range(outer), range(SHIFTS), range(GROUP), range(lanes))
+    hit = np.broadcast_to(t == SHIFTS * k + SHIFTS - 1 - r, (outer, SHIFTS, GROUP, lanes))
+    return jnp.asarray(hit.reshape(outer * SHIFTS * GROUP, lanes), jnp.bfloat16)
+
+
+def convolve(payload):
+    blocks, both, lanes = payload.shape
+    channels = both // 2
+    groups = channels // GROUP
+    outer = lanes // SHIFTS
+    return pl.pallas_call(
+        conv_kernel,
+        out_shape=jax.ShapeDtypeStruct((blocks, channels, lanes), jnp.bfloat16),
+        scratch_shapes=[
+            pltpu.VMEM((groups, SHIFTS * GROUP, blocks * lanes), jnp.bfloat16),
+            pltpu.VMEM((groups, outer * GROUP, (blocks + 1) * lanes), jnp.bfloat16),
+            pltpu.VMEM((groups, blocks * GROUP, outer * SHIFTS * GROUP), jnp.bfloat16),
+        ],
+        compiler_params=pltpu.CompilerParams(vmem_limit_bytes=24 * 2**20),
+    )(payload, placement(lanes))
+
+
+def gate_kernel(conv_ref, gate_ref, out_ref):
+    out_ref[...] = (
+        conv_ref[...].astype(jnp.float32) * gate_ref[...].astype(jnp.float32)
+    ).astype(out_ref.dtype)
+
+
+def gated(conv_t, gate_t):
+    return pl.pallas_call(
+        gate_kernel,
+        out_shape=jax.ShapeDtypeStruct(conv_t.shape, jnp.bfloat16),
+        compiler_params=pltpu.CompilerParams(vmem_limit_bytes=4 * 2**20),
+    )(conv_t, gate_t)
+
+
+def project_kernel(at_ref, own_ref, other_ref, own_weight_ref, other_weight_ref, out_ref):
+    total = lax.dot_general(
+        own_ref[...], own_weight_ref[...], TN, preferred_element_type=jnp.float32
+    )
+    total += lax.dot_general(
+        other_ref[...], other_weight_ref[...], TN, preferred_element_type=jnp.float32
+    )
+    out_ref[...] = total.astype(out_ref.dtype)
+
+
+def project(at, own, other, own_weight, other_weight, features, dtype):
+    depth, rows = own.shape
+    steps = 4
+    block = features // steps
+    return pl.pallas_call(
+        project_kernel,
+        grid_spec=pltpu.PrefetchScalarGridSpec(
+            num_scalar_prefetch=1,
+            grid=(steps,),
+            in_specs=[
+                pl.BlockSpec((depth, rows), lambda n, at: (0, 0)),
+                pl.BlockSpec((depth, rows), lambda n, at: (0, 0)),
+                pl.BlockSpec((depth, block), lambda n, at: (0, at[0] * steps + n)),
+                pl.BlockSpec((depth, block), lambda n, at: (0, at[0] * steps + n)),
+            ],
+            out_specs=pl.BlockSpec((rows, block), lambda n, at: (0, n)),
+        ),
+        out_shape=jax.ShapeDtypeStruct((rows, features), dtype),
+        compiler_params=pltpu.CompilerParams(vmem_limit_bytes=16 * 2**20),
+    )(at, own, other, own_weight, other_weight)
+
+
+def by_blocks(tokens, value_weight, gate_rows, filter_taps, out_weight):
+    peers = lax.axis_size("ctx")
+    ranks = lax.axis_size("ch")
+    rank = lax.axis_index("ch")
+    features = out_weight.shape[1] // ranks
+    near = [(i, i ^ 1) for i in range(ranks)]
+    far = [(i, i ^ 2) for i in range(ranks)]
+    other_weight = lax.ppermute(out_weight, "ch", near)
+    payload, gate_t = value_payload(tokens, value_weight, filter_taps, gate_rows, peers)
+    payload = lax.all_to_all(payload, "ctx", split_axis=0, concat_axis=0, tiled=True)
+    conv = convolve(payload)
+    conv = lax.all_to_all(conv, "ctx", split_axis=0, concat_axis=0, tiled=True)
+    own = gated(conv.reshape(gate_t.shape), gate_t)
+    other = lax.ppermute(own, "ch", near)
+    far_at, own_at = (rank ^ 2)[None], rank[None]
+    sent = project(far_at, own, other, out_weight, other_weight, features, jnp.bfloat16)
+    arrived = lax.ppermute(sent, "ch", far)
+    kept = project(own_at, own, other, out_weight, other_weight, features, jnp.float32)
+    return (kept + arrived.astype(jnp.float32)).astype(jnp.bfloat16)
+
+
+def fits_blocks(tokens, value_weight, peers, ranks):
+    rows, channels = tokens.shape[0], value_weight.shape[1]
+    return (
+        rows == LANES
+        and ranks == 4
+        and peers % 2 == 0
+        and peers <= 16
+        and channels % (peers * GROUP) == 0
+    )
+
+
+def on_device(tokens, value_weight, gate_rows, filter_taps, out_weight):
+    peers, ranks = lax.axis_size("ctx"), lax.axis_size("ch")
+    if fits_blocks(tokens, value_weight, peers, ranks):
+        return by_blocks(tokens, value_weight, gate_rows, filter_taps, out_weight)
+    return by_transform(tokens, value_weight, gate_rows, filter_taps, out_weight)
+
+
 def solution(mesh):
     placed = (P("ctx", None), P(None, "ch"), P("ctx", "ch"), P("ctx", "ch"), P("ch", None))
     return jax.shard_map(

time: 93.1 us -> 53.5 us (0.57)
  waiting for transfers between devices: 36.7 us -> 5.22 us
  blocking collectives: 0 us -> 26.9 us
  matrix products: 23 us -> 0 us
  between operations: 13.6 us -> 0.06 us
  starting transfers between devices: 14 us -> 2.11 us
  Pallas kernels: 0 us -> 10.6 us
  local copies, waits for them, and re-layouts: 4.39 us -> 7.42 us
    all_to_all x0 -> x2, blocking collectives: none -> 26.9 us  [the longest x1 16.2 us: by_blocks(): lax.all_to_all(payload, 'ctx', split_axis=0, concat_axis=0, tiled=True)]
    reduce_scatter x1 -> x0, waiting for transfers between devices: 22.8 us -> none  [on_device(): lax.psum_scatter(partial_sum.astype(jnp.bfloat16), 'ch', scatter_dimensio...]
    dot_general x18 -> x0, matrix products: 21.3 us -> none  [the longest x8 7.55 us: apply_second(): return jnp.einsum('ckb,bj->ckj', operand, table_part, precision=HIGHEST)]
    all_to_all x3 -> x0, starting transfers between devices: 14 us -> none  [the longest x1 7.25 us: on_device(): lax.all_to_all(filter_taps, 'ctx', split_axis=1, concat_axis=0, tiled=True)]
    all_to_all x3 -> x0, waiting for transfers between devices: 13.8 us -> none  [the longest x1 7.1 us: on_device(): lax.all_to_all(restored, 'ctx', split_axis=0, concat_axis=1, tiled=True)]
    pallas_call x0 -> x5, Pallas kernels: none -> 10.6 us  [the longest x2 6.03 us: project(): pl.pallas_call(project_kernel, grid_spec=pltpu.PrefetchScalarGridSpec(num...]
    unnamed x6 -> x14, local copies, waits for them, and re-layouts: 1.88 us -> 7.42 us
    ppermute x0 -> x3, waiting for transfers between devices: none -> 5.22 us  [the longest x1 3.89 us: by_blocks(): arrived = lax.ppermute(sent, 'ch', far)]
  transfers between devices with their start and end apart: 4 -> 3, of which waited for: 4 -> 2; matrix products, arithmetic and copies ran while one was open for 9% -> 0% of each run, Pallas kernels for 0% -> 14%
where the time goes in v1:
time: 53.5 us; the launch traced here: 53.1 us
  blocking collectives  26.9 us (50%)
  Pallas kernels  10.6 us (20%)
  local copies, waits for them, and re-layouts  7.42 us (14%)
  waiting for transfers between devices  5.22 us (10%)
  starting transfers between devices  2.11 us (4%)
  other arithmetic  0.76 us (1%)
    all_to_all x1, blocking collectives, by_blocks(): lax.all_to_all(payload, 'ctx', split_axis=0, concat_axis=0, tiled=True)  16.2 us
    all_to_all x1, blocking collectives, by_blocks(): conv = lax.all_to_all(conv, 'ctx', split_axis=0, concat_axis=0, tiled=True)  10.7 us
    unnamed x14, local copies, waits for them, and re-layouts  7.42 us
    pallas_call x2, Pallas kernels, project(): pl.pallas_call(project_kernel, grid_spec=pltpu.PrefetchScalarGridSpec(num...  6.03 us
    ppermute x1, waiting for transfers between devices, by_blocks(): arrived = lax.ppermute(sent, 'ch', far)  3.89 us
    pallas_call x1, Pallas kernels, convolve(): pl.pallas_call(conv_kernel, out_shape=jax.ShapeDtypeStruct((blocks, chann...  2.79 us
    pallas_call x1, Pallas kernels, value_payload(): pl.pallas_call(value_kernel, grid=(steps,), in_specs=[pl.BlockSpec((rows,...  1.78 us
    ppermute x1, starting transfers between devices, by_blocks(): arrived = lax.ppermute(sent, 'ch', far)  1.58 us
  transfers between devices with their start and end apart: 3, of which 2 were waited for; matrix products, arithmetic and copies ran while one was open for 0% of the time, Pallas kernels for 14%

profile of v1, /device:TPU:0, one launch (start us, length us, event | category | flops | bytes accessed | tf_op | source)
XLA Modules:
  0.0 53.1 jit_solution(8005877683745219752)
XLA Ops:
  0.0 0.5 collective-permute-start.1
  0.5 0.0 copy-start.2
  0.5 2.2 %copy-done.2 = bf16[4096,512]{1,0:T(8,128)(2,1)S(1)} copy-done((bf16[4096,512]{1,0:T(8,128)(2,1)S(1)}, bf16[4096,512]{1,0:T(8,128)(2,1)}, u32[]{:S(2)}) %copy-start.2) | copy-done | bytes 4194328
  2.6 0.0 copy-start.3
  2.6 1.2 %copy-done.3 = bf16[128,4096]{1,0:T(8,128)(2,1)S(1)} copy-done((bf16[128,4096]{1,0:T(8,128)(2,1)S(1)}, bf16[128,4096]{1,0:T(8,128)(2,1)}, u32[]{:S(2)}) %copy-start.3) | copy-done | bytes 1048600
  3.9 0.0 copy-start.5
  3.9 0.9 %copy-done.5 = bf16[128,512]{1,0:T(8,128)(2,1)S(1)} copy-done((bf16[128,512]{1,0:T(8,128)(2,1)S(1)}, bf16[128,512]{1,0:T(8,128)(2,1)}, u32[]{:S(2)}) %copy-start.5) | copy-done | bytes 131096
  4.8 0.0 copy-start.6
  4.8 0.9 %copy-done.6 = bf16[128,512]{1,0:T(8,128)(2,1)S(1)} copy-done((bf16[128,512]{1,0:T(8,128)(2,1)S(1)}, bf16[128,512]{1,0:T(8,128)(2,1)}, u32[]{:S(2)}) %copy-start.6) | copy-done | bytes 131096
  5.7 0.0 copy-start.4
  5.7 1.8 %shard_map.64 = (bf16[8,128,128]{2,1,0:T(8,128)(2,1)S(1)}, bf16[512,128]{1,0:T(8,128)(2,1)S(1)}) custom-call(bf16[128,4096]{1,0:T(8,128)(2,1)S(1)} %copy-done.3, bf16[4096,512]{1,0:T(8,128)(2,1)S(1)} %copy-done.2, bf16[128,512]{1,0:T(8,128)(2,1)S(1)} %copy-done.5, bf16[128,512]{1,0:T(8,128)(2,1)S(1)} %copy-done.6), custom_call_target="tpu_custom_call" | custom-call | tf_op jit(solution)/shard_map/pallas_call | solution.py:141
  7.5 16.2 %all_to_all.10.payload_ref = bf16[8,128,128]{2,1,0:T(8,128)(2,1)S(1)} all-to-all(bf16[8,128,128]{2,1,0:T(8,128)(2,1)S(1)} %get-tuple-element.7), channel_id=1, replica_groups=mesh['ctx'=8,'ch'=4] {'ctx'}, dimensions={0} | all-to-all | bytes 524288 | tf_op jit(solution)/shard_map/all_to_all | solution.py:314
  23.7 0.0 copy-done.4
  23.7 2.8 %shard_map.65 = bf16[8,64,128]{2,1,0:T(8,128)(2,1)S(1)} custom-call(bf16[8,128,128]{2,1,0:T(8,128)(2,1)S(1)} %all_to_all.10.payload_ref, bf16[2048,128]{1,0:T(8,128)(2,1)S(1)} %copy-done.4), custom_call_target="tpu_custom_call" | custom-call | tf_op jit(solution)/shard_map/pallas_call | solution.py:247
  26.5 10.7 %all_to_all.11 = bf16[8,64,128]{2,1,0:T(8,128)(2,1)S(1)} all-to-all(bf16[8,64,128]{2,1,0:T(8,128)(2,1)S(1)} %shard_map.65), channel_id=1, replica_groups=mesh['ctx'=8,'ch'=4] {'ctx'}, dimensions={0} | all-to-all | bytes 262144 | tf_op jit(solution)/shard_map/all_to_all | solution.py:316
  37.2 0.1 collective-permute-start
  37.3 1.3 %collective-permute-done.other_ref = bf16[512,128]{1,0:T(8,128)(2,1)S(1)} collective-permute-done((bf16[512,128]{1,0:T(8,128)(2,1)S(1)}, bf16[512,128]{1,0:T(8,128)(2,1)S(1)}, u32[]{:S(2)}, u32[]{:S(2)}) %collective-permute-start) | collective-permute-done | bytes 131104 | tf_op jit(solution)/shard_map/ppermute | solution.py:318
  38.6 0.0 collective-permute-done.1.other_weight_ref
  38.6 0.0 copy-start
  38.6 2.2 %copy-done = bf16[512,4096]{1,0:T(8,128)(2,1)S(1)} copy-done((bf16[512,4096]{1,0:T(8,128)(2,1)S(1)}, bf16[512,4096]{1,0:T(8,128)(2,1)}, u32[]{:S(2)}) %copy-start) | copy-done | bytes 4194328
  40.8 0.0 copy-start.1
  40.8 3.1 %shard_map.68 = bf16[128,1024]{1,0:T(8,128)(2,1)S(1)} custom-call(s32[1]{0:T(128)} %bitcast.2.at_ref, bf16[512,128]{1,0:T(8,128)(2,1)S(1)} %shard_map.66.own_ref, bf16[512,128]{1,0:T(8,128)(2,1)S(1)} %collective-permute-done.other_ref, bf16[512,4096]{1,0:T(8,128)(2,1)S(1)} %copy-done, bf16[512,4096]{1,0:T(8,128)(2,1)} %collective-permute-done.1.other_weight_ref), custom_call_target="tpu_custom_call" | custom-call | tf_op jit(solution)/shard_map/pallas_call | solution.py:287
  43.9 1.6 %collective-permute-start.2 = (bf16[128,1024]{1,0:T(8,128)(2,1)S(1)}, bf16[128,1024]{1,0:T(8,128)(2,1)S(1)}, u32[]{:S(2)}, u32[]{:S(2)}) collective-permute-start(bf16[128,1024]{1,0:T(8,128)(2,1)S(1)} %shard_map.68), channel_id=1, source_target_pairs={{0,2},{1,3},{2,0},{3,1},{4,6},{5,7},{6,4},{7,5},{8,10},{9,11},{10,... | collective-permute-start | bytes 786440 | tf_op jit(solution)/shard_map/ppermute | solution.py:321
  45.5 0.0 copy-done.1
  45.5 2.9 %shard_map.67 = f32[128,1024]{1,0:T(8,128)S(1)} custom-call(s32[1]{0:T(128)} %bitcast.at_ref, bf16[512,128]{1,0:T(8,128)(2,1)S(1)} %shard_map.66.own_ref, bf16[512,128]{1,0:T(8,128)(2,1)S(1)} %collective-permute-done.other_ref, bf16[512,4096]{1,0:T(8,128)(2,1)S(1)} %copy-done.1, bf16[512,4096]{1,0:T(8,128)(2,1)} %collective-permute-done.1.other_weight_ref), custom_call_target="tpu_custom_call" | custom-call | tf_op jit(solution)/shard_map/pallas_call | solution.py:287
  48.5 3.9 %collective-permute-done.2 = bf16[128,1024]{1,0:T(8,128)(2,1)S(1)} collective-permute-done((bf16[128,1024]{1,0:T(8,128)(2,1)S(1)}, bf16[128,1024]{1,0:T(8,128)(2,1)S(1)}, u32[]{:S(2)}, u32[]{:S(2)}) %collective-permute-start.2) | collective-permute-done | bytes 262176 | tf_op jit(solution)/shard_map/ppermute | solution.py:321
  52.4 0.8 %add_convert_fusion = bf16[128,1024]{1,0:T(8,128)(2,1)} fusion(f32[128,1024]{1,0:T(8,128)S(1)} %shard_map.67, bf16[128,1024]{1,0:T(8,128)(2,1)S(1)} %collective-permute-done.2), kind=kLoop, calls=%fused_computation | loop fusion | flops 393216 | bytes 1048576 | tf_op jit(solution)/shard_map/convert_element_type | solution.py:323
  (1 shorter events, 0.0 us)
Async XLA Ops:
  0.0 38.6 %collective-permute-start.1 = (bf16[512,4096]{1,0:T(8,128)(2,1)}, bf16[512,4096]{1,0:T(8,128)(2,1)}, u32[]{:S(2)}, u32[]{:S(2)}) collective-permute-start(bf16[512,4096]{1,0:T(8,128)(2,1)} %own_weight_ref.3), channel_id=1, source_target_pairs={{0,1},{1,0},{2,3},{3,2},{4,5},{5,4},{6,7},{7,6},{8,9},{9,8},{10,11... | collective-permute-start | bytes 12582920 | tf_op jit(solution)/shard_map/ppermute | solution.py:312
  0.5 2.2 %copy-start.2 = (bf16[4096,512]{1,0:T(8,128)(2,1)S(1)}, bf16[4096,512]{1,0:T(8,128)(2,1)}, u32[]{:S(2)}) copy-start(bf16[4096,512]{1,0:T(8,128)(2,1)} %weight_ref.1) | copy-start | bytes 12582916
  2.6 1.2 %copy-start.3 = (bf16[128,4096]{1,0:T(8,128)(2,1)S(1)}, bf16[128,4096]{1,0:T(8,128)(2,1)}, u32[]{:S(2)}) copy-start(bf16[128,4096]{1,0:T(8,128)(2,1)} %tokens_ref.1) | copy-start | bytes 3145732
  3.9 0.9 %copy-start.5 = (bf16[128,512]{1,0:T(8,128)(2,1)S(1)}, bf16[128,512]{1,0:T(8,128)(2,1)}, u32[]{:S(2)}) copy-start(bf16[128,512]{1,0:T(8,128)(2,1)} %taps_ref.1) | copy-start | bytes 393220
  4.8 0.9 %copy-start.6 = (bf16[128,512]{1,0:T(8,128)(2,1)S(1)}, bf16[128,512]{1,0:T(8,128)(2,1)}, u32[]{:S(2)}) copy-start(bf16[128,512]{1,0:T(8,128)(2,1)} %gate_ref.1) | copy-start | bytes 393220
  5.7 18.0 %copy-start.4 = (bf16[2048,128]{1,0:T(8,128)(2,1)S(1)}, bf16[2048,128]{1,0:T(8,128)(2,1)}, u32[]{:S(2)}) copy-start(bf16[2048,128]{1,0:T(8,128)(2,1)} %constant.8.clone.place_ref) | copy-start | bytes 1572868
  37.2 1.4 %collective-permute-start = (bf16[512,128]{1,0:T(8,128)(2,1)S(1)}, bf16[512,128]{1,0:T(8,128)(2,1)S(1)}, u32[]{:S(2)}, u32[]{:S(2)}) collective-permute-start(bf16[512,128]{1,0:T(8,128)(2,1)S(1)} %shard_map.66.own_ref), channel_id=1, source_target_pairs={{0,1},{1,0},{2,3},{3,2},{4,5},{5,4},{6,7},{7,6},{8,9},{9,8},{10,11... | collective-permute-start | bytes 393224 | tf_op jit(solution)/shard_map/ppermute | solution.py:318
  38.6 2.2 %copy-start = (bf16[512,4096]{1,0:T(8,128)(2,1)S(1)}, bf16[512,4096]{1,0:T(8,128)(2,1)}, u32[]{:S(2)}) copy-start(bf16[512,4096]{1,0:T(8,128)(2,1)} %own_weight_ref.3) | copy-start | bytes 12582916
  40.8 4.7 %copy-start.1 = (bf16[512,4096]{1,0:T(8,128)(2,1)S(1)}, bf16[512,4096]{1,0:T(8,128)(2,1)}, u32[]{:S(2)}) copy-start(bf16[512,4096]{1,0:T(8,128)(2,1)} %own_weight_ref.3) | copy-start | bytes 12582916
  43.9 8.4 %collective-permute-start.2 = (bf16[128,1024]{1,0:T(8,128)(2,1)S(1)}, bf16[128,1024]{1,0:T(8,128)(2,1)S(1)}, u32[]{:S(2)}, u32[]{:S(2)}) collective-permute-start(bf16[128,1024]{1,0:T(8,128)(2,1)S(1)} %shard_map.68), channel_id=1, source_target_pairs={{0,2},{1,3},{2,0},{3,1},{4,6},{5,7},{6,4},{7,5},{8,10},{9,11},{10,... | collective-permute-start | bytes 786440 | tf_op jit(solution)/shard_map/ppermute | solution.py:321

commit v2 on v1

--- a/solution.py
+++ b/solution.py
@@ -1,3 +1,4 @@
+import functools
 import math
 
 import jax
@@ -105,59 +106,31 @@
 TN = (((0,), (0,)), ((), ()))
 
 
-def value_kernel(tokens_ref, weight_ref, taps_ref, gate_ref, payload_ref, gate_t_ref, total_ref):
-    step = pl.program_id(0)
+def turn_kernel(value_ref, taps_ref, gate_ref, payload_ref, gate_t_ref):
     peers, both, rows = payload_ref.shape
     part = both // 2
-
-    @pl.when(step == 0)
-    def _():
-        total_ref[...] = jnp.zeros_like(total_ref)
-        row = lax.broadcasted_iota(jnp.int32, (rows, rows), 0)
-        column = lax.broadcasted_iota(jnp.int32, (rows, rows), 1)
-        flip = jnp.where(row + column == rows - 1, 1.0, 0.0).astype(jnp.bfloat16)
-        flipped = jnp.dot(flip, taps_ref[...], preferred_element_type=jnp.float32)
-        flipped_t = flipped.T.astype(jnp.bfloat16)
-        for peer in range(peers):
-            payload_ref[peer, part:, :] = flipped_t[peer * part : (peer + 1) * part]
-        gate_t_ref[...] = gate_ref[...].astype(jnp.float32).T.astype(jnp.bfloat16)
-
-    total_ref[...] += jnp.dot(
-        tokens_ref[...], weight_ref[...], preferred_element_type=jnp.float32
-    )
-
-    @pl.when(step == pl.num_programs(0) - 1)
-    def _():
-        value_t = total_ref[...].T.astype(jnp.bfloat16)
-        for peer in range(peers):
-            payload_ref[peer, :part, :] = value_t[peer * part : (peer + 1) * part]
-
-
-def value_payload(tokens, value_weight, filter_taps, gate_rows, peers):
-    rows, depth = tokens.shape
-    channels = value_weight.shape[1]
-    steps = 4
-    block = depth // steps
+    row = lax.broadcasted_iota(jnp.int32, (rows, rows), 0)
+    column = lax.broadcasted_iota(jnp.int32, (rows, rows), 1)
+    flip = jnp.where(row + column == rows - 1, 1.0, 0.0).astype(jnp.bfloat16)
+    flipped = jnp.dot(flip, taps_ref[...], preferred_element_type=jnp.float32)
+    flipped_t = flipped.T.astype(jnp.bfloat16)
+    value_t = value_ref[...].astype(jnp.float32).T.astype(jnp.bfloat16)
+    for peer in range(peers):
+        payload_ref[peer, :part, :] = value_t[peer * part : (peer + 1) * part]
+        payload_ref[peer, part:, :] = flipped_t[peer * part : (peer + 1) * part]
+    gate_t_ref[...] = gate_ref[...].astype(jnp.float32).T.astype(jnp.bfloat16)
+
+
+def turned(value, filter_taps, gate_rows, peers):
+    rows, channels = value.shape
     return pl.pallas_call(
-        value_kernel,
-        grid=(steps,),
-        in_specs=[
-            pl.BlockSpec((rows, block), lambda k: (0, k)),
-            pl.BlockSpec((block, channels), lambda k: (k, 0)),
-            pl.BlockSpec((rows, channels), lambda k: (0, 0)),
-            pl.BlockSpec((rows, channels), lambda k: (0, 0)),
-        ],
-        out_specs=[
-            pl.BlockSpec((peers, 2 * channels // peers, rows), lambda k: (0, 0, 0)),
-            pl.BlockSpec((channels, rows), lambda k: (0, 0)),
-        ],
+        turn_kernel,
         out_shape=[
             jax.ShapeDtypeStruct((peers, 2 * channels // peers, rows), jnp.bfloat16),
             jax.ShapeDtypeStruct((channels, rows), jnp.bfloat16),
         ],
-        scratch_shapes=[pltpu.VMEM((rows, channels), jnp.float32)],
-        compiler_params=pltpu.CompilerParams(vmem_limit_bytes=16 * 2**20),
-    )(tokens, value_weight, filter_taps, gate_rows)
+        compiler_params=pltpu.CompilerParams(vmem_limit_bytes=8 * 2**20),
+    )(value, filter_taps, gate_rows)
 
 
 def conv_kernel(payload_ref, place_ref, out_ref, value_ref, taps_ref, picked_ref):
@@ -203,18 +176,18 @@
             )
         taps_ref[group, :, length:] = jnp.zeros((outer * GROUP, lanes), jnp.bfloat16)
         for pair in range(blocks // 2):
-            depth = 2 * lanes * (pair + 1)
+            span = 2 * lanes * (pair + 1)
             even = (blocks - 1 - 2 * pair) * lanes
             odd = even - lanes
             left_side = jnp.concatenate(
                 [
-                    taps_ref[group, :, even : even + depth],
-                    taps_ref[group, :, odd : odd + depth],
+                    taps_ref[group, :, even : even + span],
+                    taps_ref[group, :, odd : odd + span],
                 ],
                 axis=0,
             )
             mixed = lax.dot_general(
-                left_side, value_ref[group, :, :depth], NT, preferred_element_type=jnp.float32
+                left_side, value_ref[group, :, :span], NT, preferred_element_type=jnp.float32
             )
             picked = jnp.where(same, mixed, 0.0).astype(jnp.bfloat16)
             for half in range(2):
@@ -252,6 +225,11 @@
             pltpu.VMEM((groups, outer * GROUP, (blocks + 1) * lanes), jnp.bfloat16),
             pltpu.VMEM((groups, blocks * GROUP, outer * SHIFTS * GROUP), jnp.bfloat16),
         ],
+        cost_estimate=pl.CostEstimate(
+            flops=2 * channels * GROUP * (blocks * lanes) ** 2,
+            bytes_accessed=6 * channels * blocks * lanes,
+            transcendentals=0,
+        ),
         compiler_params=pltpu.CompilerParams(vmem_limit_bytes=24 * 2**20),
     )(payload, placement(lanes))
 
@@ -270,56 +248,46 @@
     )(conv_t, gate_t)
 
 
-def project_kernel(at_ref, own_ref, other_ref, own_weight_ref, other_weight_ref, out_ref):
+def project_kernel(far, own_ref, other_ref, own_weight_ref, other_weight_ref, out_ref):
+    features = out_ref.shape[1]
+    rank = lax.axis_index("ch") ^ (2 if far else 0)
+    span = pl.ds(pl.multiple_of(rank * features, features), features)
     total = lax.dot_general(
-        own_ref[...], own_weight_ref[...], TN, preferred_element_type=jnp.float32
+        own_ref[...], own_weight_ref[:, span], TN, preferred_element_type=jnp.float32
     )
     total += lax.dot_general(
-        other_ref[...], other_weight_ref[...], TN, preferred_element_type=jnp.float32
+        other_ref[...], other_weight_ref[:, span], TN, preferred_element_type=jnp.float32
     )
     out_ref[...] = total.astype(out_ref.dtype)
 
 
-def project(at, own, other, own_weight, other_weight, features, dtype):
-    depth, rows = own.shape
-    steps = 4
-    block = features // steps
+def project(own, other, own_weight, other_weight, features, far, dtype):
     return pl.pallas_call(
-        project_kernel,
-        grid_spec=pltpu.PrefetchScalarGridSpec(
-            num_scalar_prefetch=1,
-            grid=(steps,),
-            in_specs=[
-                pl.BlockSpec((depth, rows), lambda n, at: (0, 0)),
-                pl.BlockSpec((depth, rows), lambda n, at: (0, 0)),
-                pl.BlockSpec((depth, block), lambda n, at: (0, at[0] * steps + n)),
-                pl.BlockSpec((depth, block), lambda n, at: (0, at[0] * steps + n)),
-            ],
-            out_specs=pl.BlockSpec((rows, block), lambda n, at: (0, n)),
-        ),
-        out_shape=jax.ShapeDtypeStruct((rows, features), dtype),
-        compiler_params=pltpu.CompilerParams(vmem_limit_bytes=16 * 2**20),
-    )(at, own, other, own_weight, other_weight)
+        functools.partial(project_kernel, far),
+        out_shape=jax.ShapeDtypeStruct((own.shape[1], features), dtype),
+        compiler_params=pltpu.CompilerParams(vmem_limit_bytes=24 * 2**20),
+    )(own, other, own_weight, other_weight)
 
 
 def by_blocks(tokens, value_weight, gate_rows, filter_taps, out_weight):
     peers = lax.axis_size("ctx")
     ranks = lax.axis_size("ch")
-    rank = lax.axis_index("ch")
     features = out_weight.shape[1] // ranks
     near = [(i, i ^ 1) for i in range(ranks)]
     far = [(i, i ^ 2) for i in range(ranks)]
+    value = jnp.dot(tokens, value_weight, preferred_element_type=jnp.float32).astype(
+        jnp.bfloat16
+    )
+    payload, gate_t = turned(value, filter_taps, gate_rows, peers)
     other_weight = lax.ppermute(out_weight, "ch", near)
-    payload, gate_t = value_payload(tokens, value_weight, filter_taps, gate_rows, peers)
     payload = lax.all_to_all(payload, "ctx", split_axis=0, concat_axis=0, tiled=True)
     conv = convolve(payload)
     conv = lax.all_to_all(conv, "ctx", split_axis=0, concat_axis=0, tiled=True)
     own = gated(conv.reshape(gate_t.shape), gate_t)
     other = lax.ppermute(own, "ch", near)
-    far_at, own_at = (rank ^ 2)[None], rank[None]
-    sent = project(far_at, own, other, out_weight, other_weight, features, jnp.bfloat16)
+    sent = project(own, other, out_weight, other_weight, features, True, jnp.bfloat16)
     arrived = lax.ppermute(sent, "ch", far)
-    kept = project(own_at, own, other, out_weight, other_weight, features, jnp.float32)
+    kept = project(own, other, out_weight, other_weight, features, False, jnp.float32)
     return (kept + arrived.astype(jnp.float32)).astype(jnp.bfloat16)
 
 

time: 53.5 us -> 45.4 us (0.85)
  local copies, waits for them, and re-layouts: 7.42 us -> 0.83 us
  Pallas kernels: 10.6 us -> 4.04 us
  matrix products: 0 us -> 2.9 us
  waiting for transfers between devices: 5.22 us -> 7.71 us
    pallas_call x3, Pallas kernels: 7.81 us -> 1.21 us  [the longest x2 0.94 us: project(): pl.pallas_call(functools.partial(project_kernel, far), out_shape=jax.Shap...]
    unnamed x14 -> x10, local copies, waits for them, and re-layouts: 7.42 us -> 0.83 us
    dot_general x0 -> x1, matrix products: none -> 2.9 us  [by_blocks(): jnp.dot(tokens, value_weight, preferred_element_type=jnp.float32)]
    ppermute x1, waiting for transfers between devices: 3.89 us -> 6.37 us  [by_blocks(): arrived = lax.ppermute(sent, 'ch', far)]
  transfers between devices with their start and end apart: 3 -> 3, of which waited for: 2 -> 2; matrix products, arithmetic and copies ran while one was open for 0% -> 6% of each run, Pallas kernels for 14% -> 8%
where the time goes in v2:
time: 45.4 us; the launch traced here: 45.2 us
  blocking collectives  26.7 us (59%)
  waiting for transfers between devices  7.71 us (17%)
  Pallas kernels  4.04 us (9%)
  matrix products  2.9 us (6%)
  starting transfers between devices  2.18 us (5%)
  local copies, waits for them, and re-layouts  0.83 us (2%)
  other arithmetic  0.76 us (2%)
    all_to_all x1, blocking collectives, by_blocks(): lax.all_to_all(payload, 'ctx', split_axis=0, concat_axis=0, tiled=True)  16 us
    all_to_all x1, blocking collectives, by_blocks(): conv = lax.all_to_all(conv, 'ctx', split_axis=0, concat_axis=0, tiled=True)  10.7 us
    ppermute x1, waiting for transfers between devices, by_blocks(): arrived = lax.ppermute(sent, 'ch', far)  6.37 us
    dot_general x1, matrix products, by_blocks(): jnp.dot(tokens, value_weight, preferred_element_type=jnp.float32)  2.9 us
    pallas_call x1, Pallas kernels, convolve(): pl.pallas_call(conv_kernel, out_shape=jax.ShapeDtypeStruct((blocks, chann...  2.79 us
    ppermute x1, starting transfers between devices, by_blocks(): arrived = lax.ppermute(sent, 'ch', far)  1.58 us
    ppermute x1, waiting for transfers between devices, by_blocks(): other = lax.ppermute(own, 'ch', near)  1.33 us
    pallas_call x2, Pallas kernels, project(): pl.pallas_call(functools.partial(project_kernel, far), out_shape=jax.Shap...  0.94 us
  transfers between devices with their start and end apart: 3, of which 2 were waited for; matrix products, arithmetic and copies ran while one was open for 6% of the time, Pallas kernels for 8%

profile of v2, /device:TPU:0, one launch (start us, length us, event | category | flops | bytes accessed | tf_op | source)
XLA Modules:
  0.0 45.2 jit_solution(1971021431458013189)
XLA Ops:
  0.0 0.0 copy-start
  0.0 0.0 copy-start.4
  0.0 0.0 copy-start.2
  0.0 0.0 copy-start.3
  0.0 0.5 %collective-permute-start.1 = (bf16[512,4096]{1,0:T(8,128)(2,1)}, bf16[512,4096]{1,0:T(8,128)(2,1)S(1)}, u32[]{:S(2)}, u32[]{:S(2)}) collective-permute-start(bf16[512,4096]{1,0:T(8,128)(2,1)} %own_weight_ref.3), channel_id=1, source_target_pairs={{0,1},{1,0},{2,3},{3,2},{4,5},{5,4},{6,7},{7,6},{8,9},{9,8},{10,11... | collective-permute-start | bytes 12582920 | tf_op jit(solution)/shard_map/ppermute | solution.py:282
  0.5 0.8 %copy-done = bf16[128,4096]{1,0:T(8,128)(2,1)S(1)} copy-done((bf16[128,4096]{1,0:T(8,128)(2,1)S(1)}, bf16[128,4096]{1,0:T(8,128)(2,1)}, u32[]{:S(2)}) %copy-start) | copy-done | bytes 1048600
  1.4 2.9 %convolution_convert_fusion.value_ref = bf16[128,512]{1,0:T(8,128)(2,1)S(1)} fusion(bf16[128,4096]{1,0:T(8,128)(2,1)S(1)} %copy-done, bf16[4096,512]{1,0:T(8,128)(2,1)} %param.7), kind=kOutput, calls=%fused_computation | convolution fusion | flops 536936448 | bytes 5373952 | tf_op jit(solution)/shard_map/dot_general | solution.py:278
  4.3 0.0 copy-done.2
  4.3 0.0 copy-done.3
  4.3 0.3 shard_map.64
  4.6 16.0 %all_to_all.10.payload_ref = bf16[8,128,128]{2,1,0:T(8,128)(2,1)S(1)} all-to-all(bf16[8,128,128]{2,1,0:T(8,128)(2,1)S(1)} %get-tuple-element.7), channel_id=1, replica_groups=mesh['ctx'=8,'ch'=4] {'ctx'}, dimensions={0} | all-to-all | bytes 524288 | tf_op jit(solution)/shard_map/all_to_all | solution.py:283
  20.5 0.0 copy-done.4
  20.5 0.0 copy-start.1
  20.5 2.8 %shard_map.65 = bf16[8,64,128]{2,1,0:T(8,128)(2,1)S(1)} custom-call(bf16[8,128,128]{2,1,0:T(8,128)(2,1)S(1)} %all_to_all.10.payload_ref, bf16[2048,128]{1,0:T(8,128)(2,1)S(1)} %copy-done.4), custom_call_target="tpu_custom_call" | custom-call | flops 2147483648 | bytes 393216 | tf_op jit(solution)/shard_map/pallas_call | solution.py:220
  23.3 10.7 %all_to_all.11 = bf16[8,64,128]{2,1,0:T(8,128)(2,1)S(1)} all-to-all(bf16[8,64,128]{2,1,0:T(8,128)(2,1)S(1)} %shard_map.65), channel_id=1, replica_groups=mesh['ctx'=8,'ch'=4] {'ctx'}, dimensions={0} | all-to-all | bytes 262144 | tf_op jit(solution)/shard_map/all_to_all | solution.py:285
  34.1 0.1 collective-permute-start
  34.2 1.3 %collective-permute-done.other_ref = bf16[512,128]{1,0:T(8,128)(2,1)S(1)} collective-permute-done((bf16[512,128]{1,0:T(8,128)(2,1)S(1)}, bf16[512,128]{1,0:T(8,128)(2,1)S(1)}, u32[]{:S(2)}, u32[]{:S(2)}) %collective-permute-start) | collective-permute-done | bytes 131104 | tf_op jit(solution)/shard_map/ppermute | solution.py:287
  35.5 0.0 collective-permute-done.1.other_weight_ref
  35.5 0.0 copy-done.1
  35.5 0.5 %shard_map.68 = bf16[128,1024]{1,0:T(8,128)(2,1)S(1)} custom-call(bf16[512,128]{1,0:T(8,128)(2,1)S(1)} %shard_map.66.own_ref, bf16[512,128]{1,0:T(8,128)(2,1)S(1)} %collective-permute-done.other_ref, bf16[512,4096]{1,0:T(8,128)(2,1)S(1)} %copy-done.1, bf16[512,4096]{1,0:T(8,128)(2,1)S(1)} %collective-permute-done.1.other_weight_ref), custom_call_target="tpu_custom_call" | custom-call | tf_op jit(solution)/shard_map/pallas_call | solution.py:265
  36.0 1.6 %collective-permute-start.2 = (bf16[128,1024]{1,0:T(8,128)(2,1)S(1)}, bf16[128,1024]{1,0:T(8,128)(2,1)S(1)}, u32[]{:S(2)}, u32[]{:S(2)}) collective-permute-start(bf16[128,1024]{1,0:T(8,128)(2,1)S(1)} %shard_map.68), channel_id=1, source_target_pairs={{0,2},{1,3},{2,0},{3,1},{4,6},{5,7},{6,4},{7,5},{8,10},{9,11},{10,... | collective-permute-start | bytes 786440 | tf_op jit(solution)/shard_map/ppermute | solution.py:289
  37.6 0.5 %shard_map.67 = f32[128,1024]{1,0:T(8,128)S(1)} custom-call(bf16[512,128]{1,0:T(8,128)(2,1)S(1)} %shard_map.66.own_ref, bf16[512,128]{1,0:T(8,128)(2,1)S(1)} %collective-permute-done.other_ref, bf16[512,4096]{1,0:T(8,128)(2,1)S(1)} %copy-done.1, bf16[512,4096]{1,0:T(8,128)(2,1)S(1)} %collective-permute-done.1.other_weight_ref), custom_call_target="tpu_custom_call" | custom-call | tf_op jit(solution)/shard_map/pallas_call | solution.py:265
  38.1 6.4 %collective-permute-done.2 = bf16[128,1024]{1,0:T(8,128)(2,1)S(1)} collective-permute-done((bf16[128,1024]{1,0:T(8,128)(2,1)S(1)}, bf16[128,1024]{1,0:T(8,128)(2,1)S(1)}, u32[]{:S(2)}, u32[]{:S(2)}) %collective-permute-start.2) | collective-permute-done | bytes 262176 | tf_op jit(solution)/shard_map/ppermute | solution.py:289
  44.4 0.8 %add_convert_fusion = bf16[128,1024]{1,0:T(8,128)(2,1)} fusion(f32[128,1024]{1,0:T(8,128)S(1)} %shard_map.67, bf16[128,1024]{1,0:T(8,128)(2,1)S(1)} %collective-permute-done.2), kind=kLoop, calls=%fused_computation.1 | loop fusion | flops 393216 | bytes 1048576 | tf_op jit(solution)/shard_map/convert_element_type | solution.py:291
  (1 shorter events, 0.0 us)
Async XLA Ops:
  0.0 1.4 %copy-start = (bf16[128,4096]{1,0:T(8,128)(2,1)S(1)}, bf16[128,4096]{1,0:T(8,128)(2,1)}, u32[]{:S(2)}) copy-start(bf16[128,4096]{1,0:T(8,128)(2,1)} %param.6) | copy-start | bytes 3145732
  0.0 20.5 %copy-start.4 = (bf16[2048,128]{1,0:T(8,128)(2,1)S(1)}, bf16[2048,128]{1,0:T(8,128)(2,1)}, u32[]{:S(2)}) copy-start(bf16[2048,128]{1,0:T(8,128)(2,1)} %constant.2.clone.place_ref) | copy-start | bytes 1572868
  0.0 4.3 %copy-start.2 = (bf16[128,512]{1,0:T(8,128)(2,1)S(1)}, bf16[128,512]{1,0:T(8,128)(2,1)}, u32[]{:S(2)}) copy-start(bf16[128,512]{1,0:T(8,128)(2,1)} %taps_ref.1) | copy-start | bytes 393220
  0.0 4.3 %copy-start.3 = (bf16[128,512]{1,0:T(8,128)(2,1)S(1)}, bf16[128,512]{1,0:T(8,128)(2,1)}, u32[]{:S(2)}) copy-start(bf16[128,512]{1,0:T(8,128)(2,1)} %gate_ref.1) | copy-start | bytes 393220
  0.0 35.5 %collective-permute-start.1 = (bf16[512,4096]{1,0:T(8,128)(2,1)}, bf16[512,4096]{1,0:T(8,128)(2,1)S(1)}, u32[]{:S(2)}, u32[]{:S(2)}) collective-permute-start(bf16[512,4096]{1,0:T(8,128)(2,1)} %own_weight_ref.3), channel_id=1, source_target_pairs={{0,1},{1,0},{2,3},{3,2},{4,5},{5,4},{6,7},{7,6},{8,9},{9,8},{10,11... | collective-permute-start | bytes 12582920 | tf_op jit(solution)/shard_map/ppermute | solution.py:282
  20.5 15.0 %copy-start.1 = (bf16[512,4096]{1,0:T(8,128)(2,1)S(1)}, bf16[512,4096]{1,0:T(8,128)(2,1)}, u32[]{:S(2)}) copy-start(bf16[512,4096]{1,0:T(8,128)(2,1)} %own_weight_ref.3) | copy-start | bytes 12582916
  34.1 1.4 %collective-permute-start = (bf16[512,128]{1,0:T(8,128)(2,1)S(1)}, bf16[512,128]{1,0:T(8,128)(2,1)S(1)}, u32[]{:S(2)}, u32[]{:S(2)}) collective-permute-start(bf16[512,128]{1,0:T(8,128)(2,1)S(1)} %shard_map.66.own_ref), channel_id=1, source_target_pairs={{0,1},{1,0},{2,3},{3,2},{4,5},{5,4},{6,7},{7,6},{8,9},{9,8},{10,11... | collective-permute-start | bytes 393224 | tf_op jit(solution)/shard_map/ppermute | solution.py:287
  36.0 8.4 %collective-permute-start.2 = (bf16[128,1024]{1,0:T(8,128)(2,1)S(1)}, bf16[128,1024]{1,0:T(8,128)(2,1)S(1)}, u32[]{:S(2)}, u32[]{:S(2)}) collective-permute-start(bf16[128,1024]{1,0:T(8,128)(2,1)S(1)} %shard_map.68), channel_id=1, source_target_pairs={{0,2},{1,3},{2,0},{3,1},{4,6},{5,7},{6,4},{7,5},{8,10},{9,11},{10,... | collective-permute-start | bytes 786440 | tf_op jit(solution)/shard_map/ppermute | solution.py:289

commit v3 on v2

--- a/solution.py
+++ b/solution.py
@@ -114,7 +114,18 @@
     flip = jnp.where(row + column == rows - 1, 1.0, 0.0).astype(jnp.bfloat16)
     flipped = jnp.dot(flip, taps_ref[...], preferred_element_type=jnp.float32)
     flipped_t = flipped.T.astype(jnp.bfloat16)
-    value_t = value_ref[...].astype(jnp.float32).T.astype(jnp.bfloat16)
+    mirror = jnp.where(
+        (row // GROUP == column // GROUP) & (row % GROUP + column % GROUP == GROUP - 1), 1.0, 0.0
+    ).astype(jnp.bfloat16)
+    value_t = jnp.concatenate(
+        [
+            lax.dot_general(
+                mirror, value_ref[:, at : at + rows], NT, preferred_element_type=jnp.float32
+            )
+            for at in range(0, value_ref.shape[1], rows)
+        ],
+        axis=0,
+    ).astype(jnp.bfloat16)
     for peer in range(peers):
         payload_ref[peer, :part, :] = value_t[peer * part : (peer + 1) * part]
         payload_ref[peer, part:, :] = flipped_t[peer * part : (peer + 1) * part]
@@ -133,16 +144,14 @@
     )(value, filter_taps, gate_rows)
 
 
-def conv_kernel(payload_ref, place_ref, out_ref, value_ref, taps_ref, picked_ref):
+def conv_kernel(payload_ref, place_ref, out_ref, value_ref, taps_ref, packed_ref):
     blocks, both, lanes = payload_ref.shape
     channels = both // 2
     length = blocks * lanes
     outer = lanes // SHIFTS
     tail = jnp.zeros((GROUP, lanes), jnp.float32)
-    rows = 2 * outer * GROUP
-    row = lax.broadcasted_iota(jnp.int32, (rows, SHIFTS * GROUP), 0)
-    column = lax.broadcasted_iota(jnp.int32, (rows, SHIFTS * GROUP), 1)
-    same = row % GROUP == column % GROUP
+    sides = SHIFTS * GROUP // lanes
+    slot = lax.broadcasted_iota(jnp.int32, (GROUP, lanes), 1) % GROUP
     for group in range(channels // GROUP):
         first = group * GROUP
         padded = jnp.concatenate(
@@ -189,27 +198,34 @@
             mixed = lax.dot_general(
                 left_side, value_ref[group, :, :span], NT, preferred_element_type=jnp.float32
             )
-            picked = jnp.where(same, mixed, 0.0).astype(jnp.bfloat16)
             for half in range(2):
-                block = 2 * pair + half
-                for k in range(outer):
-                    at = (half * outer + k) * GROUP
-                    picked_ref[
-                        group,
-                        block * GROUP : (block + 1) * GROUP,
-                        k * SHIFTS * GROUP : (k + 1) * SHIFTS * GROUP,
-                    ] = picked[at : at + GROUP]
-        result = jnp.dot(picked_ref[group], place_ref[...], preferred_element_type=jnp.float32)
-        result = result.astype(jnp.bfloat16)
+                for side in range(sides):
+                    packed = None
+                    for k in range(outer):
+                        at = (half * outer + k) * GROUP
+                        tile = mixed[at : at + GROUP, side * lanes : (side + 1) * lanes]
+                        tile = pltpu.roll(tile, k + 1, 1, stride=1, stride_axis=0)
+                        packed = tile if k == 0 else jnp.where(slot == k, tile, packed)
+                    at = (group * blocks + 2 * pair + half) * GROUP
+                    packed_ref[at : at + GROUP, side * lanes : (side + 1) * lanes] = packed.astype(
+                        jnp.bfloat16
+                    )
+    result = jnp.dot(packed_ref[...], place_ref[...], preferred_element_type=jnp.float32)
+    result = result.astype(jnp.bfloat16)
+    for group in range(channels // GROUP):
         for block in range(blocks):
-            out_ref[block, first : first + GROUP, :] = result[block * GROUP : (block + 1) * GROUP]
+            at = (group * blocks + block) * GROUP
+            out_ref[block, group * GROUP : (group + 1) * GROUP, :] = result[at : at + GROUP]
 
 
 def placement(lanes):
-    outer = lanes // SHIFTS
-    k, r, _, t = np.ix_(range(outer), range(SHIFTS), range(GROUP), range(lanes))
-    hit = np.broadcast_to(t == SHIFTS * k + SHIFTS - 1 - r, (outer, SHIFTS, GROUP, lanes))
-    return jnp.asarray(hit.reshape(outer * SHIFTS * GROUP, lanes), jnp.bfloat16)
+    per_side = lanes // GROUP
+    side, place, slot, t = np.ix_(
+        range(SHIFTS // per_side), range(per_side), range(GROUP), range(lanes)
+    )
+    r = side * per_side + (place - 1) % per_side
+    hit = t == SHIFTS * slot + SHIFTS - 1 - r
+    return jnp.asarray(hit.reshape(SHIFTS * GROUP, lanes), jnp.bfloat16)
 
 
 def convolve(payload):
@@ -223,7 +239,7 @@
         scratch_shapes=[
             pltpu.VMEM((groups, SHIFTS * GROUP, blocks * lanes), jnp.bfloat16),
             pltpu.VMEM((groups, outer * GROUP, (blocks + 1) * lanes), jnp.bfloat16),
-            pltpu.VMEM((groups, blocks * GROUP, outer * SHIFTS * GROUP), jnp.bfloat16),
+            pltpu.VMEM((groups * blocks * GROUP, SHIFTS * GROUP), jnp.bfloat16),
         ],
         cost_estimate=pl.CostEstimate(
             flops=2 * channels * GROUP * (blocks * lanes) ** 2,

time: 45.4 us -> 44.8 us (0.987)
  Pallas kernels: 4.04 us -> 3.43 us
    pallas_call x1, Pallas kernels: 2.79 us -> 2.17 us  [convolve(): pl.pallas_call(conv_kernel, out_shape=jax.ShapeDtypeStruct((blocks, chann...]
  transfers between devices with their start and end apart: 3 -> 3, of which waited for: 2 -> 2; matrix products, arithmetic and copies ran while one was open for 6% -> 7% of each run, Pallas kernels for 8% -> 7%
where the time goes in v3:
time: 44.8 us; the launch traced here: 44.6 us
  blocking collectives  26.7 us (60%)
  waiting for transfers between devices  7.71 us (17%)
  Pallas kernels  3.43 us (8%)
  matrix products  2.9 us (6%)
  starting transfers between devices  2.18 us (5%)
  local copies, waits for them, and re-layouts  0.83 us (2%)
  other arithmetic  0.76 us (2%)
    all_to_all x1, blocking collectives, by_blocks(): lax.all_to_all(payload, 'ctx', split_axis=0, concat_axis=0, tiled=True)  16 us
    all_to_all x1, blocking collectives, by_blocks(): conv = lax.all_to_all(conv, 'ctx', split_axis=0, concat_axis=0, tiled=True)  10.7 us
    ppermute x1, waiting for transfers between devices, by_blocks(): arrived = lax.ppermute(sent, 'ch', far)  6.37 us
    dot_general x1, matrix products, by_blocks(): jnp.dot(tokens, value_weight, preferred_element_type=jnp.float32)  2.9 us
    pallas_call x1, Pallas kernels, convolve(): pl.pallas_call(conv_kernel, out_shape=jax.ShapeDtypeStruct((blocks, chann...  2.17 us
    ppermute x1, starting transfers between devices, by_blocks(): arrived = lax.ppermute(sent, 'ch', far)  1.58 us
    ppermute x1, waiting for transfers between devices, by_blocks(): other = lax.ppermute(own, 'ch', near)  1.33 us
    pallas_call x2, Pallas kernels, project(): pl.pallas_call(functools.partial(project_kernel, far), out_shape=jax.Shap...  0.93 us
  transfers between devices with their start and end apart: 3, of which 2 were waited for; matrix products, arithmetic and copies ran while one was open for 7% of the time, Pallas kernels for 7%

profile of v3, /device:TPU:0, one launch (start us, length us, event | category | flops | bytes accessed | tf_op | source)
XLA Modules:
  0.0 44.6 jit_solution(12003619250174985177)
XLA Ops:
  0.0 0.0 copy-start
  0.0 0.0 copy-start.4
  0.0 0.0 copy-start.2
  0.0 0.0 copy-start.3
  0.0 0.5 %collective-permute-start.1 = (bf16[512,4096]{1,0:T(8,128)(2,1)}, bf16[512,4096]{1,0:T(8,128)(2,1)S(1)}, u32[]{:S(2)}, u32[]{:S(2)}) collective-permute-start(bf16[512,4096]{1,0:T(8,128)(2,1)} %own_weight_ref.3), channel_id=1, source_target_pairs={{0,1},{1,0},{2,3},{3,2},{4,5},{5,4},{6,7},{7,6},{8,9},{9,8},{10,11... | collective-permute-start | bytes 12582920 | tf_op jit(solution)/shard_map/ppermute | solution.py:298
  0.5 0.8 %copy-done = bf16[128,4096]{1,0:T(8,128)(2,1)S(1)} copy-done((bf16[128,4096]{1,0:T(8,128)(2,1)S(1)}, bf16[128,4096]{1,0:T(8,128)(2,1)}, u32[]{:S(2)}) %copy-start) | copy-done | bytes 1048600
  1.4 2.9 %convolution_convert_fusion.value_ref = bf16[128,512]{1,0:T(8,128)(2,1)S(1)} fusion(bf16[128,4096]{1,0:T(8,128)(2,1)S(1)} %copy-done, bf16[4096,512]{1,0:T(8,128)(2,1)} %param.7), kind=kOutput, calls=%fused_computation | convolution fusion | flops 536936448 | bytes 5373952 | tf_op jit(solution)/shard_map/dot_general | solution.py:294
  4.3 0.0 copy-done.2
  4.3 0.0 copy-done.3
  4.3 0.3 shard_map.64
  4.6 16.0 %all_to_all.10.payload_ref = bf16[8,128,128]{2,1,0:T(8,128)(2,1)S(1)} all-to-all(bf16[8,128,128]{2,1,0:T(8,128)(2,1)S(1)} %get-tuple-element.7), channel_id=1, replica_groups=mesh['ctx'=8,'ch'=4] {'ctx'}, dimensions={0} | all-to-all | bytes 524288 | tf_op jit(solution)/shard_map/all_to_all | solution.py:299
  20.5 0.0 copy-done.4
  20.5 0.0 copy-start.1
  20.5 2.2 %shard_map.65 = bf16[8,64,128]{2,1,0:T(8,128)(2,1)S(1)} custom-call(bf16[8,128,128]{2,1,0:T(8,128)(2,1)S(1)} %all_to_all.10.payload_ref, bf16[256,128]{1,0:T(8,128)(2,1)S(1)} %copy-done.4), custom_call_target="tpu_custom_call" | custom-call | flops 2147483648 | bytes 393216 | tf_op jit(solution)/shard_map/pallas_call | solution.py:236
  22.7 10.7 %all_to_all.11 = bf16[8,64,128]{2,1,0:T(8,128)(2,1)S(1)} all-to-all(bf16[8,64,128]{2,1,0:T(8,128)(2,1)S(1)} %shard_map.65), channel_id=1, replica_groups=mesh['ctx'=8,'ch'=4] {'ctx'}, dimensions={0} | all-to-all | bytes 262144 | tf_op jit(solution)/shard_map/all_to_all | solution.py:301
  33.5 0.1 collective-permute-start
  33.6 1.3 %collective-permute-done.other_ref = bf16[512,128]{1,0:T(8,128)(2,1)S(1)} collective-permute-done((bf16[512,128]{1,0:T(8,128)(2,1)S(1)}, bf16[512,128]{1,0:T(8,128)(2,1)S(1)}, u32[]{:S(2)}, u32[]{:S(2)}) %collective-permute-start) | collective-permute-done | bytes 131104 | tf_op jit(solution)/shard_map/ppermute | solution.py:303
  34.9 0.0 collective-permute-done.1.other_weight_ref
  34.9 0.0 copy-done.1
  34.9 0.5 %shard_map.68 = bf16[128,1024]{1,0:T(8,128)(2,1)S(1)} custom-call(bf16[512,128]{1,0:T(8,128)(2,1)S(1)} %shard_map.66.own_ref, bf16[512,128]{1,0:T(8,128)(2,1)S(1)} %collective-permute-done.other_ref, bf16[512,4096]{1,0:T(8,128)(2,1)S(1)} %copy-done.1, bf16[512,4096]{1,0:T(8,128)(2,1)S(1)} %collective-permute-done.1.other_weight_ref), custom_call_target="tpu_custom_call" | custom-call | tf_op jit(solution)/shard_map/pallas_call | solution.py:281
  35.4 1.6 %collective-permute-start.2 = (bf16[128,1024]{1,0:T(8,128)(2,1)S(1)}, bf16[128,1024]{1,0:T(8,128)(2,1)S(1)}, u32[]{:S(2)}, u32[]{:S(2)}) collective-permute-start(bf16[128,1024]{1,0:T(8,128)(2,1)S(1)} %shard_map.68), channel_id=1, source_target_pairs={{0,2},{1,3},{2,0},{3,1},{4,6},{5,7},{6,4},{7,5},{8,10},{9,11},{10,... | collective-permute-start | bytes 786440 | tf_op jit(solution)/shard_map/ppermute | solution.py:305
  37.0 0.5 %shard_map.67 = f32[128,1024]{1,0:T(8,128)S(1)} custom-call(bf16[512,128]{1,0:T(8,128)(2,1)S(1)} %shard_map.66.own_ref, bf16[512,128]{1,0:T(8,128)(2,1)S(1)} %collective-permute-done.other_ref, bf16[512,4096]{1,0:T(8,128)(2,1)S(1)} %copy-done.1, bf16[512,4096]{1,0:T(8,128)(2,1)S(1)} %collective-permute-done.1.other_weight_ref), custom_call_target="tpu_custom_call" | custom-call | tf_op jit(solution)/shard_map/pallas_call | solution.py:281
  37.4 6.4 %collective-permute-done.2 = bf16[128,1024]{1,0:T(8,128)(2,1)S(1)} collective-permute-done((bf16[128,1024]{1,0:T(8,128)(2,1)S(1)}, bf16[128,1024]{1,0:T(8,128)(2,1)S(1)}, u32[]{:S(2)}, u32[]{:S(2)}) %collective-permute-start.2) | collective-permute-done | bytes 262176 | tf_op jit(solution)/shard_map/ppermute | solution.py:305
  43.8 0.8 %add_convert_fusion = bf16[128,1024]{1,0:T(8,128)(2,1)} fusion(f32[128,1024]{1,0:T(8,128)S(1)} %shard_map.67, bf16[128,1024]{1,0:T(8,128)(2,1)S(1)} %collective-permute-done.2), kind=kLoop, calls=%fused_computation.1 | loop fusion | flops 393216 | bytes 1048576 | tf_op jit(solution)/shard_map/convert_element_type | solution.py:307
  (1 shorter events, 0.0 us)
Async XLA Ops:
  0.0 1.4 %copy-start = (bf16[128,4096]{1,0:T(8,128)(2,1)S(1)}, bf16[128,4096]{1,0:T(8,128)(2,1)}, u32[]{:S(2)}) copy-start(bf16[128,4096]{1,0:T(8,128)(2,1)} %param.6) | copy-start | bytes 3145732
  0.0 20.5 %copy-start.4 = (bf16[256,128]{1,0:T(8,128)(2,1)S(1)}, bf16[256,128]{1,0:T(8,128)(2,1)}, u32[]{:S(2)}) copy-start(bf16[256,128]{1,0:T(8,128)(2,1)} %constant.2.clone.place_ref) | copy-start | bytes 196612
  0.0 4.3 %copy-start.2 = (bf16[128,512]{1,0:T(8,128)(2,1)S(1)}, bf16[128,512]{1,0:T(8,128)(2,1)}, u32[]{:S(2)}) copy-start(bf16[128,512]{1,0:T(8,128)(2,1)} %taps_ref.1) | copy-start | bytes 393220
  0.0 4.3 %copy-start.3 = (bf16[128,512]{1,0:T(8,128)(2,1)S(1)}, bf16[128,512]{1,0:T(8,128)(2,1)}, u32[]{:S(2)}) copy-start(bf16[128,512]{1,0:T(8,128)(2,1)} %gate_ref.1) | copy-start | bytes 393220
  0.0 34.9 %collective-permute-start.1 = (bf16[512,4096]{1,0:T(8,128)(2,1)}, bf16[512,4096]{1,0:T(8,128)(2,1)S(1)}, u32[]{:S(2)}, u32[]{:S(2)}) collective-permute-start(bf16[512,4096]{1,0:T(8,128)(2,1)} %own_weight_ref.3), channel_id=1, source_target_pairs={{0,1},{1,0},{2,3},{3,2},{4,5},{5,4},{6,7},{7,6},{8,9},{9,8},{10,11... | collective-permute-start | bytes 12582920 | tf_op jit(solution)/shard_map/ppermute | solution.py:298
  20.5 14.4 %copy-start.1 = (bf16[512,4096]{1,0:T(8,128)(2,1)S(1)}, bf16[512,4096]{1,0:T(8,128)(2,1)}, u32[]{:S(2)}) copy-start(bf16[512,4096]{1,0:T(8,128)(2,1)} %own_weight_ref.3) | copy-start | bytes 12582916
  33.5 1.4 %collective-permute-start = (bf16[512,128]{1,0:T(8,128)(2,1)S(1)}, bf16[512,128]{1,0:T(8,128)(2,1)S(1)}, u32[]{:S(2)}, u32[]{:S(2)}) collective-permute-start(bf16[512,128]{1,0:T(8,128)(2,1)S(1)} %shard_map.66.own_ref), channel_id=1, source_target_pairs={{0,1},{1,0},{2,3},{3,2},{4,5},{5,4},{6,7},{7,6},{8,9},{9,8},{10,11... | collective-permute-start | bytes 393224 | tf_op jit(solution)/shard_map/ppermute | solution.py:303
  35.4 8.4 %collective-permute-start.2 = (bf16[128,1024]{1,0:T(8,128)(2,1)S(1)}, bf16[128,1024]{1,0:T(8,128)(2,1)S(1)}, u32[]{:S(2)}, u32[]{:S(2)}) collective-permute-start(bf16[128,1024]{1,0:T(8,128)(2,1)S(1)} %shard_map.68), channel_id=1, source_target_pairs={{0,2},{1,3},{2,0},{3,1},{4,6},{5,7},{6,4},{7,5},{8,10},{9,11},{10,... | collective-permute-start | bytes 786440 | tf_op jit(solution)/shard_map/ppermute | solution.py:305

commit v4 on v3

--- a/solution.py
+++ b/solution.py
@@ -152,7 +152,7 @@
     tail = jnp.zeros((GROUP, lanes), jnp.float32)
     sides = SHIFTS * GROUP // lanes
     slot = lax.broadcasted_iota(jnp.int32, (GROUP, lanes), 1) % GROUP
-    for group in range(channels // GROUP):
+    def build(group):
         first = group * GROUP
         padded = jnp.concatenate(
             [
@@ -184,6 +184,8 @@
                 jnp.bfloat16
             )
         taps_ref[group, :, length:] = jnp.zeros((outer * GROUP, lanes), jnp.bfloat16)
+
+    def mix(group):
         for pair in range(blocks // 2):
             span = 2 * lanes * (pair + 1)
             even = (blocks - 1 - 2 * pair) * lanes
@@ -210,6 +212,13 @@
                     packed_ref[at : at + GROUP, side * lanes : (side + 1) * lanes] = packed.astype(
                         jnp.bfloat16
                     )
+
+    groups = channels // GROUP
+    build(0)
+    for group in range(groups):
+        if group + 1 < groups:
+            build(group + 1)
+        mix(group)
     result = jnp.dot(packed_ref[...], place_ref[...], preferred_element_type=jnp.float32)
     result = result.astype(jnp.bfloat16)
     for group in range(channels // GROUP):
@@ -264,25 +273,41 @@
     )(conv_t, gate_t)
 
 
-def project_kernel(far, own_ref, other_ref, own_weight_ref, other_weight_ref, out_ref):
+def project_kernel(flip, own_ref, weight_ref, out_ref):
     features = out_ref.shape[1]
-    rank = lax.axis_index("ch") ^ (2 if far else 0)
-    span = pl.ds(pl.multiple_of(rank * features, features), features)
-    total = lax.dot_general(
-        own_ref[...], own_weight_ref[:, span], TN, preferred_element_type=jnp.float32
-    )
-    total += lax.dot_general(
-        other_ref[...], other_weight_ref[:, span], TN, preferred_element_type=jnp.float32
-    )
-    out_ref[...] = total.astype(out_ref.dtype)
-
-
-def project(own, other, own_weight, other_weight, features, far, dtype):
-    return pl.pallas_call(
-        functools.partial(project_kernel, far),
-        out_shape=jax.ShapeDtypeStruct((own.shape[1], features), dtype),
+    at = (lax.axis_index("ch") ^ flip) * features
+    out_ref[...] = lax.dot_general(
+        own_ref[...],
+        weight_ref[:, pl.ds(pl.multiple_of(at, features), features)],
+        TN,
+        preferred_element_type=jnp.float32,
+    ).astype(out_ref.dtype)
+
+
+def project(own, weight, features, flip, dtype):
+    depth, rows = own.shape
+    return pl.pallas_call(
+        functools.partial(project_kernel, flip),
+        out_shape=jax.ShapeDtypeStruct((rows, features), dtype),
+        cost_estimate=pl.CostEstimate(
+            flops=2 * rows * depth * features,
+            bytes_accessed=2 * depth * features + 4 * rows * features,
+            transcendentals=0,
+        ),
         compiler_params=pltpu.CompilerParams(vmem_limit_bytes=24 * 2**20),
-    )(own, other, own_weight, other_weight)
+    )(own, weight)
+
+
+def add_kernel(first_ref, second_ref, out_ref):
+    out_ref[...] = (first_ref[...] + second_ref[...].astype(jnp.float32)).astype(out_ref.dtype)
+
+
+def added(first, second):
+    return pl.pallas_call(
+        add_kernel,
+        out_shape=jax.ShapeDtypeStruct(first.shape, jnp.bfloat16),
+        compiler_params=pltpu.CompilerParams(vmem_limit_bytes=8 * 2**20),
+    )(first, second)
 
 
 def by_blocks(tokens, value_weight, gate_rows, filter_taps, out_weight):
@@ -295,16 +320,19 @@
         jnp.bfloat16
     )
     payload, gate_t = turned(value, filter_taps, gate_rows, peers)
-    other_weight = lax.ppermute(out_weight, "ch", near)
     payload = lax.all_to_all(payload, "ctx", split_axis=0, concat_axis=0, tiled=True)
     conv = convolve(payload)
     conv = lax.all_to_all(conv, "ctx", split_axis=0, concat_axis=0, tiled=True)
     own = gated(conv.reshape(gate_t.shape), gate_t)
-    other = lax.ppermute(own, "ch", near)
-    sent = project(own, other, out_weight, other_weight, features, True, jnp.bfloat16)
+    far_near = lax.ppermute(project(own, out_weight, features, 3, jnp.bfloat16), "ch", near)
+    far_own = project(own, out_weight, features, 2, jnp.float32)
+    sent = added(far_own, far_near)
     arrived = lax.ppermute(sent, "ch", far)
-    kept = project(own, other, out_weight, other_weight, features, False, jnp.float32)
-    return (kept + arrived.astype(jnp.float32)).astype(jnp.bfloat16)
+    kept_near = lax.ppermute(project(own, out_weight, features, 1, jnp.bfloat16), "ch", near)
+    kept = project(own, out_weight, features, 0, jnp.float32)
+    return (
+        kept + kept_near.astype(jnp.float32) + arrived.astype(jnp.float32)
+    ).astype(jnp.bfloat16)
 
 
 def fits_blocks(tokens, value_weight, peers, ranks):

time: 44.8 us -> 44.8 us (level)
  waiting for transfers between devices: 7.71 us -> 6.78 us
  local copies, waits for them, and re-layouts: 0.83 us -> 1.36 us
    ppermute x2, waiting for transfers between devices: 1.34 us -> 0.29 us  [the longest x1 0.29 us: by_blocks(): lax.ppermute(project(own, out_weight, features, 3, jnp.bfloat16), 'ch', n...]
    unnamed x10, local copies, waits for them, and re-layouts: 0.83 us -> 1.36 us
    pallas_call x2 -> x5, Pallas kernels: 0.93 us -> 1.36 us  [the longest x4 1.32 us: project(): pl.pallas_call(functools.partial(project_kernel, flip), out_shape=jax.Sha...]
  transfers between devices with their start and end apart: 3 -> 3, of which waited for: 2 -> 2; matrix products, arithmetic and copies ran while one was open for 7% -> 0% of each run, Pallas kernels for 7% -> 2%
where the time goes in v4:
time: 44.8 us; the launch traced here: 44.6 us
  blocking collectives  26.7 us (60%)
  waiting for transfers between devices  6.78 us (15%)
  Pallas kernels  3.77 us (8%)
  matrix products  2.9 us (6%)
  starting transfers between devices  2.21 us (5%)
  local copies, waits for them, and re-layouts  1.36 us (3%)
  other arithmetic  0.8 us (2%)
    all_to_all x1, blocking collectives, by_blocks(): lax.all_to_all(payload, 'ctx', split_axis=0, concat_axis=0, tiled=True)  16 us
    all_to_all x1, blocking collectives, by_blocks(): conv = lax.all_to_all(conv, 'ctx', split_axis=0, concat_axis=0, tiled=True)  10.7 us
    ppermute x1, waiting for transfers between devices, by_blocks(): arrived = lax.ppermute(sent, 'ch', far)  6.49 us
    dot_general x1, matrix products, by_blocks(): jnp.dot(tokens, value_weight, preferred_element_type=jnp.float32)  2.9 us
    pallas_call x1, Pallas kernels, convolve(): pl.pallas_call(conv_kernel, out_shape=jax.ShapeDtypeStruct((blocks, chann...  2.09 us
    ppermute x1, starting transfers between devices, by_blocks(): arrived = lax.ppermute(sent, 'ch', far)  1.58 us
    unnamed x10, local copies, waits for them, and re-layouts  1.36 us
    pallas_call x4, Pallas kernels, project(): pl.pallas_call(functools.partial(project_kernel, flip), out_shape=jax.Sha...  1.32 us
  transfers between devices with their start and end apart: 3, of which 2 were waited for; matrix products, arithmetic and copies ran while one was open for 0% of the time, Pallas kernels for 2%

profile of v4, /device:TPU:0, one launch (start us, length us, event | category | flops | bytes accessed | tf_op | source)
XLA Modules:
  0.0 44.6 jit_solution(236228550561035783)
XLA Ops:
  0.0 0.0 copy-start
  0.0 0.0 copy-start.4
  0.0 0.0 copy-start.3
  0.0 0.0 copy-start.2
  0.0 1.3 %copy-done = bf16[128,4096]{1,0:T(8,128)(2,1)S(1)} copy-done((bf16[128,4096]{1,0:T(8,128)(2,1)S(1)}, bf16[128,4096]{1,0:T(8,128)(2,1)}, u32[]{:S(2)}) %copy-start) | copy-done | bytes 1048600
  1.4 2.9 %convolution_convert_fusion.value_ref = bf16[128,512]{1,0:T(8,128)(2,1)S(1)} fusion(bf16[128,4096]{1,0:T(8,128)(2,1)S(1)} %copy-done, bf16[4096,512]{1,0:T(8,128)(2,1)} %param.7), kind=kOutput, calls=%fused_computation | convolution fusion | flops 536936448 | bytes 5373952 | tf_op jit(solution)/shard_map/dot_general | solution.py:319
  4.3 0.0 copy-done.3
  4.3 0.0 copy-done.2
  4.3 0.3 shard_map.64
  4.6 16.0 %all_to_all.10.payload_ref = bf16[8,128,128]{2,1,0:T(8,128)(2,1)S(1)} all-to-all(bf16[8,128,128]{2,1,0:T(8,128)(2,1)S(1)} %get-tuple-element.7), channel_id=1, replica_groups=mesh['ctx'=8,'ch'=4] {'ctx'}, dimensions={0} | all-to-all | bytes 524288 | tf_op jit(solution)/shard_map/all_to_all | solution.py:323
  20.5 0.0 copy-done.4
  20.5 0.0 copy-start.1
  20.5 2.1 %shard_map.65 = bf16[8,64,128]{2,1,0:T(8,128)(2,1)S(1)} custom-call(bf16[8,128,128]{2,1,0:T(8,128)(2,1)S(1)} %all_to_all.10.payload_ref, bf16[256,128]{1,0:T(8,128)(2,1)S(1)} %copy-done.4), custom_call_target="tpu_custom_call" | custom-call | flops 2147483648 | bytes 393216 | tf_op jit(solution)/shard_map/pallas_call | solution.py:245
  22.6 10.7 %all_to_all.11 = bf16[8,64,128]{2,1,0:T(8,128)(2,1)S(1)} all-to-all(bf16[8,64,128]{2,1,0:T(8,128)(2,1)S(1)} %shard_map.65), channel_id=1, replica_groups=mesh['ctx'=8,'ch'=4] {'ctx'}, dimensions={0} | all-to-all | bytes 262144 | tf_op jit(solution)/shard_map/all_to_all | solution.py:325
  33.4 0.0 copy-done.1
  33.4 0.3 shard_map.70
  33.7 0.1 collective-permute-start.1
  33.8 0.3 shard_map.68
  34.2 0.6 %collective-permute-start = (bf16[128,1024]{1,0:T(8,128)(2,1)S(1)}, bf16[128,1024]{1,0:T(8,128)(2,1)S(1)}, u32[]{:S(2)}, u32[]{:S(2)}) collective-permute-start(bf16[128,1024]{1,0:T(8,128)(2,1)S(1)} %shard_map.68), channel_id=1, source_target_pairs={{0,1},{1,0},{2,3},{3,2},{4,5},{5,4},{6,7},{7,6},{8,9},{9,8},{10,11... | collective-permute-start | bytes 786440 | tf_op jit(solution)/shard_map/ppermute | solution.py:331
  34.7 0.3 shard_map.69.first_ref
  35.0 0.3 collective-permute-done.1.second_ref
  35.4 1.6 %collective-permute-start.2 = (bf16[128,1024]{1,0:T(8,128)(2,1)S(1)}, bf16[128,1024]{1,0:T(8,128)(2,1)S(1)}, u32[]{:S(2)}, u32[]{:S(2)}) collective-permute-start(bf16[128,1024]{1,0:T(8,128)(2,1)S(1)} %shard_map.71), channel_id=1, source_target_pairs={{0,2},{1,3},{2,0},{3,1},{4,6},{5,7},{6,4},{7,5},{8,10},{9,11},{10,... | collective-permute-start | bytes 786440 | tf_op jit(solution)/shard_map/ppermute | solution.py:330
  37.0 0.3 shard_map.67
  37.3 0.0 collective-permute-done
  37.3 6.5 %collective-permute-done.2 = bf16[128,1024]{1,0:T(8,128)(2,1)S(1)} collective-permute-done((bf16[128,1024]{1,0:T(8,128)(2,1)S(1)}, bf16[128,1024]{1,0:T(8,128)(2,1)S(1)}, u32[]{:S(2)}, u32[]{:S(2)}) %collective-permute-start.2) | collective-permute-done | bytes 262176 | tf_op jit(solution)/shard_map/ppermute | solution.py:330
  43.8 0.8 %add_convert_fusion = bf16[128,1024]{1,0:T(8,128)(2,1)} fusion(bf16[128,1024]{1,0:T(8,128)(2,1)S(1)} %collective-permute-done.2, f32[128,1024]{1,0:T(8,128)S(1)} %shard_map.67, bf16[128,1024]{1,0:T(8,128)(2,1)S(1)} %collective-permute-done), kind=kLoop, calls=%fused_computation.1 | loop fusion | flops 655360 | bytes 1310720 | tf_op jit(solution)/shard_map/convert_element_type | solution.py:335
  (2 shorter events, 0.1 us)
Async XLA Ops:
  0.0 1.4 %copy-start = (bf16[128,4096]{1,0:T(8,128)(2,1)S(1)}, bf16[128,4096]{1,0:T(8,128)(2,1)}, u32[]{:S(2)}) copy-start(bf16[128,4096]{1,0:T(8,128)(2,1)} %param.6) | copy-start | bytes 3145732
  0.0 20.5 %copy-start.4 = (bf16[256,128]{1,0:T(8,128)(2,1)S(1)}, bf16[256,128]{1,0:T(8,128)(2,1)}, u32[]{:S(2)}) copy-start(bf16[256,128]{1,0:T(8,128)(2,1)} %constant.2.clone.place_ref) | copy-start | bytes 196612
  0.0 4.3 %copy-start.3 = (bf16[128,512]{1,0:T(8,128)(2,1)S(1)}, bf16[128,512]{1,0:T(8,128)(2,1)}, u32[]{:S(2)}) copy-start(bf16[128,512]{1,0:T(8,128)(2,1)} %gate_ref.1) | copy-start | bytes 393220
  0.0 4.3 %copy-start.2 = (bf16[128,512]{1,0:T(8,128)(2,1)S(1)}, bf16[128,512]{1,0:T(8,128)(2,1)}, u32[]{:S(2)}) copy-start(bf16[128,512]{1,0:T(8,128)(2,1)} %taps_ref.1) | copy-start | bytes 393220
  20.5 12.8 %copy-start.1 = (bf16[512,4096]{1,0:T(8,128)(2,1)S(1)}, bf16[512,4096]{1,0:T(8,128)(2,1)}, u32[]{:S(2)}) copy-start(bf16[512,4096]{1,0:T(8,128)(2,1)} %weight_ref.7) | copy-start | bytes 12582916
  33.7 1.6 %collective-permute-start.1 = (bf16[128,1024]{1,0:T(8,128)(2,1)S(1)}, bf16[128,1024]{1,0:T(8,128)(2,1)S(1)}, u32[]{:S(2)}, u32[]{:S(2)}) collective-permute-start(bf16[128,1024]{1,0:T(8,128)(2,1)S(1)} %shard_map.70), channel_id=1, source_target_pairs={{0,1},{1,0},{2,3},{3,2},{4,5},{5,4},{6,7},{7,6},{8,9},{9,8},{10,11... | collective-permute-start | bytes 786440 | tf_op jit(solution)/shard_map/ppermute | solution.py:327
  34.2 3.1 %collective-permute-start = (bf16[128,1024]{1,0:T(8,128)(2,1)S(1)}, bf16[128,1024]{1,0:T(8,128)(2,1)S(1)}, u32[]{:S(2)}, u32[]{:S(2)}) collective-permute-start(bf16[128,1024]{1,0:T(8,128)(2,1)S(1)} %shard_map.68), channel_id=1, source_target_pairs={{0,1},{1,0},{2,3},{3,2},{4,5},{5,4},{6,7},{7,6},{8,9},{9,8},{10,11... | collective-permute-start | bytes 786440 | tf_op jit(solution)/shard_map/ppermute | solution.py:331
  35.4 8.4 %collective-permute-start.2 = (bf16[128,1024]{1,0:T(8,128)(2,1)S(1)}, bf16[128,1024]{1,0:T(8,128)(2,1)S(1)}, u32[]{:S(2)}, u32[]{:S(2)}) collective-permute-start(bf16[128,1024]{1,0:T(8,128)(2,1)S(1)} %shard_map.71), channel_id=1, source_target_pairs={{0,2},{1,3},{2,0},{3,1},{4,6},{5,7},{6,4},{7,5},{8,10},{9,11},{10,... | collective-permute-start | bytes 786440 | tf_op jit(solution)/shard_map/ppermute | solution.py:330

commit v5 on v4

--- a/solution.py
+++ b/solution.py
@@ -102,25 +102,42 @@
 LANES = 128
 SHIFTS = 16
 GROUP = 16
+AHEAD_FLOPS = 4 * 2**30
 NT = (((1,), (1,)), ((), ()))
 TN = (((0,), (0,)), ((), ()))
 
 
-def turn_kernel(value_ref, taps_ref, gate_ref, payload_ref, gate_t_ref):
+def orders_kernel(flip_ref, mirror_ref):
+    rows = flip_ref.shape[0]
+    row = lax.broadcasted_iota(jnp.int32, (rows, rows), 0)
+    column = lax.broadcasted_iota(jnp.int32, (rows, rows), 1)
+    flip_ref[...] = jnp.where(row + column == rows - 1, 1.0, 0.0).astype(jnp.bfloat16)
+    mirror_ref[...] = jnp.where(
+        (row // GROUP == column // GROUP) & (row % GROUP + column % GROUP == GROUP - 1), 1.0, 0.0
+    ).astype(jnp.bfloat16)
+
+
+def orders(rows):
+    shape = jax.ShapeDtypeStruct((rows, rows), jnp.bfloat16)
+    return pl.pallas_call(
+        orders_kernel,
+        out_shape=[shape, shape],
+        cost_estimate=pl.CostEstimate(
+            flops=AHEAD_FLOPS, bytes_accessed=4 * rows * rows, transcendentals=0
+        ),
+        compiler_params=pltpu.CompilerParams(vmem_limit_bytes=4 * 2**20),
+    )()
+
+
+def turn_kernel(flip_ref, mirror_ref, value_ref, taps_ref, gate_ref, payload_ref, gate_t_ref):
     peers, both, rows = payload_ref.shape
     part = both // 2
-    row = lax.broadcasted_iota(jnp.int32, (rows, rows), 0)
-    column = lax.broadcasted_iota(jnp.int32, (rows, rows), 1)
-    flip = jnp.where(row + column == rows - 1, 1.0, 0.0).astype(jnp.bfloat16)
-    flipped = jnp.dot(flip, taps_ref[...], preferred_element_type=jnp.float32)
+    flipped = jnp.dot(flip_ref[...], taps_ref[...], preferred_element_type=jnp.float32)
     flipped_t = flipped.T.astype(jnp.bfloat16)
-    mirror = jnp.where(
-        (row // GROUP == column // GROUP) & (row % GROUP + column % GROUP == GROUP - 1), 1.0, 0.0
-    ).astype(jnp.bfloat16)
     value_t = jnp.concatenate(
         [
             lax.dot_general(
-                mirror, value_ref[:, at : at + rows], NT, preferred_element_type=jnp.float32
+                mirror_ref[...], value_ref[:, at : at + rows], NT, preferred_element_type=jnp.float32
             )
             for at in range(0, value_ref.shape[1], rows)
         ],
@@ -132,7 +149,7 @@
     gate_t_ref[...] = gate_ref[...].astype(jnp.float32).T.astype(jnp.bfloat16)
 
 
-def turned(value, filter_taps, gate_rows, peers):
+def turned(flip, mirror, value, filter_taps, gate_rows, peers):
     rows, channels = value.shape
     return pl.pallas_call(
         turn_kernel,
@@ -141,7 +158,7 @@
             jax.ShapeDtypeStruct((channels, rows), jnp.bfloat16),
         ],
         compiler_params=pltpu.CompilerParams(vmem_limit_bytes=8 * 2**20),
-    )(value, filter_taps, gate_rows)
+    )(flip, mirror, value, filter_taps, gate_rows)
 
 
 def conv_kernel(payload_ref, place_ref, out_ref, value_ref, taps_ref, packed_ref):
@@ -316,10 +333,14 @@
     features = out_weight.shape[1] // ranks
     near = [(i, i ^ 1) for i in range(ranks)]
     far = [(i, i ^ 2) for i in range(ranks)]
+    flip, mirror = orders(tokens.shape[0])
+    flip, tokens, value_weight, filter_taps, gate_rows = lax.optimization_barrier(
+        (flip, tokens, value_weight, filter_taps, gate_rows)
+    )
     value = jnp.dot(tokens, value_weight, preferred_element_type=jnp.float32).astype(
         jnp.bfloat16
     )
-    payload, gate_t = turned(value, filter_taps, gate_rows, peers)
+    payload, gate_t = turned(flip, mirror, value, filter_taps, gate_rows, peers)
     payload = lax.all_to_all(payload, "ctx", split_axis=0, concat_axis=0, tiled=True)
     conv = convolve(payload)
     conv = lax.all_to_all(conv, "ctx", split_axis=0, concat_axis=0, tiled=True)

time: 44.8 us -> 43.8 us (0.978)
  matrix products: 2.9 us -> 0.77 us
  local copies, waits for them, and re-layouts: 1.36 us -> 2.46 us
    dot_general x1, matrix products: 2.9 us -> 0.77 us  [by_blocks(): jnp.dot(tokens, value_weight, preferred_element_type=jnp.float32)]
    unnamed x10 -> x12, local copies, waits for them, and re-layouts: 1.36 us -> 2.46 us
where the time goes in v5:
time: 43.8 us; the launch traced here: 43.6 us
  blocking collectives  26.7 us (61%)
  waiting for transfers between devices  6.78 us (15%)
  Pallas kernels  3.79 us (9%)
  local copies, waits for them, and re-layouts  2.46 us (6%)
  starting transfers between devices  2.21 us (5%)
  other arithmetic  0.8 us (2%)
  matrix products  0.77 us (2%)
    all_to_all x1, blocking collectives, by_blocks(): lax.all_to_all(payload, 'ctx', split_axis=0, concat_axis=0, tiled=True)  16 us
    all_to_all x1, blocking collectives, by_blocks(): conv = lax.all_to_all(conv, 'ctx', split_axis=0, concat_axis=0, tiled=True)  10.7 us
    ppermute x1, waiting for transfers between devices, by_blocks(): arrived = lax.ppermute(sent, 'ch', far)  6.49 us
    unnamed x12, local copies, waits for them, and re-layouts  2.46 us
    pallas_call x1, Pallas kernels, convolve(): pl.pallas_call(conv_kernel, out_shape=jax.ShapeDtypeStruct((blocks, chann...  2.09 us
    ppermute x1, starting transfers between devices, by_blocks(): arrived = lax.ppermute(sent, 'ch', far)  1.58 us
    pallas_call x4, Pallas kernels, project(): pl.pallas_call(functools.partial(project_kernel, flip), out_shape=jax.Sha...  1.32 us
  transfers between devices with their start and end apart: 3, of which 2 were waited for; matrix products, arithmetic and copies ran while one was open for 0% of the time, Pallas kernels for 2%

profile of v5, /device:TPU:0, one launch (start us, length us, event | category | flops | bytes accessed | tf_op | source)
XLA Modules:
  0.0 43.6 jit_solution(9733680272406179055)
XLA Ops:
  0.0 0.0 copy-start
  0.0 0.0 copy-start.5
  0.0 0.0 copy-start.2
  0.1 0.0 copy-start.3
  0.1 0.0 copy-start.4
  0.1 1.1 %copy-done = bf16[128,4096]{1,0:T(8,128)(2,1)S(1)} copy-done((bf16[128,4096]{1,0:T(8,128)(2,1)S(1)}, bf16[128,4096]{1,0:T(8,128)(2,1)}, u32[]{:S(2)}) %copy-start) | copy-done | bytes 1048600
  1.2 1.3 %copy-done.5 = bf16[4096,512]{1,0:T(8,128)(2,1)S(1)} copy-done((bf16[4096,512]{1,0:T(8,128)(2,1)S(1)}, bf16[4096,512]{1,0:T(8,128)(2,1)}, u32[]{:S(2)}) %copy-start.5) | copy-done | bytes 4194328
  2.5 0.8 %convolution_convert_fusion.value_ref = bf16[128,512]{1,0:T(8,128)(2,1)S(1)} fusion(bf16[128,4096]{1,0:T(8,128)(2,1)S(1)} %copy-done, bf16[4096,512]{1,0:T(8,128)(2,1)S(1)} %copy-done.5), kind=kOutput, calls=%fused_computation | convolution fusion | flops 536936448 | bytes 5373952 | tf_op jit(solution)/shard_map/dot_general | solution.py:340
  3.3 0.0 copy-done.2
  3.3 0.0 copy-done.3
  3.3 0.3 shard_map.65
  3.6 16.0 %all_to_all.10.payload_ref = bf16[8,128,128]{2,1,0:T(8,128)(2,1)S(1)} all-to-all(bf16[8,128,128]{2,1,0:T(8,128)(2,1)S(1)} %get-tuple-element.21), channel_id=1, replica_groups=mesh['ctx'=8,'ch'=4] {'ctx'}, dimensions={0} | all-to-all | bytes 524288 | tf_op jit(solution)/shard_map/all_to_all | solution.py:344
  19.6 0.0 copy-done.4
  19.6 0.0 copy-start.1
  19.6 2.1 %shard_map.66 = bf16[8,64,128]{2,1,0:T(8,128)(2,1)S(1)} custom-call(bf16[8,128,128]{2,1,0:T(8,128)(2,1)S(1)} %all_to_all.10.payload_ref, bf16[256,128]{1,0:T(8,128)(2,1)S(1)} %copy-done.4), custom_call_target="tpu_custom_call" | custom-call | flops 2147483648 | bytes 393216 | tf_op jit(solution)/shard_map/pallas_call | solution.py:262
  21.7 10.7 %all_to_all.11 = bf16[8,64,128]{2,1,0:T(8,128)(2,1)S(1)} all-to-all(bf16[8,64,128]{2,1,0:T(8,128)(2,1)S(1)} %shard_map.66), channel_id=1, replica_groups=mesh['ctx'=8,'ch'=4] {'ctx'}, dimensions={0} | all-to-all | bytes 262144 | tf_op jit(solution)/shard_map/all_to_all | solution.py:346
  32.4 0.0 copy-done.1
  32.4 0.3 shard_map.71
  32.8 0.1 collective-permute-start.1
  32.8 0.3 shard_map.69
  33.2 0.6 %collective-permute-start = (bf16[128,1024]{1,0:T(8,128)(2,1)S(1)}, bf16[128,1024]{1,0:T(8,128)(2,1)S(1)}, u32[]{:S(2)}, u32[]{:S(2)}) collective-permute-start(bf16[128,1024]{1,0:T(8,128)(2,1)S(1)} %shard_map.69), channel_id=1, source_target_pairs={{0,1},{1,0},{2,3},{3,2},{4,5},{5,4},{6,7},{7,6},{8,9},{9,8},{10,11... | collective-permute-start | bytes 786440 | tf_op jit(solution)/shard_map/ppermute | solution.py:352
  33.7 0.3 shard_map.70.first_ref
  34.1 0.3 collective-permute-done.1.second_ref
  34.4 1.6 %collective-permute-start.2 = (bf16[128,1024]{1,0:T(8,128)(2,1)S(1)}, bf16[128,1024]{1,0:T(8,128)(2,1)S(1)}, u32[]{:S(2)}, u32[]{:S(2)}) collective-permute-start(bf16[128,1024]{1,0:T(8,128)(2,1)S(1)} %shard_map.72), channel_id=1, source_target_pairs={{0,2},{1,3},{2,0},{3,1},{4,6},{5,7},{6,4},{7,5},{8,10},{9,11},{10,... | collective-permute-start | bytes 786440 | tf_op jit(solution)/shard_map/ppermute | solution.py:351
  36.0 0.3 shard_map.68
  36.3 0.0 collective-permute-done
  36.3 6.5 %collective-permute-done.2 = bf16[128,1024]{1,0:T(8,128)(2,1)S(1)} collective-permute-done((bf16[128,1024]{1,0:T(8,128)(2,1)S(1)}, bf16[128,1024]{1,0:T(8,128)(2,1)S(1)}, u32[]{:S(2)}, u32[]{:S(2)}) %collective-permute-start.2) | collective-permute-done | bytes 262176 | tf_op jit(solution)/shard_map/ppermute | solution.py:351
  42.8 0.8 %add_convert_fusion = bf16[128,1024]{1,0:T(8,128)(2,1)} fusion(bf16[128,1024]{1,0:T(8,128)(2,1)S(1)} %collective-permute-done.2, f32[128,1024]{1,0:T(8,128)S(1)} %shard_map.68, bf16[128,1024]{1,0:T(8,128)(2,1)S(1)} %collective-permute-done), kind=kLoop, calls=%fused_computation.1 | loop fusion | flops 655360 | bytes 1310720 | tf_op jit(solution)/shard_map/convert_element_type | solution.py:356
  (3 shorter events, 0.1 us)
Async XLA Ops:
  0.0 1.2 %copy-start = (bf16[128,4096]{1,0:T(8,128)(2,1)S(1)}, bf16[128,4096]{1,0:T(8,128)(2,1)}, u32[]{:S(2)}) copy-start(bf16[128,4096]{1,0:T(8,128)(2,1)} %param.6) | copy-start | bytes 3145732
  0.0 2.5 %copy-start.5 = (bf16[4096,512]{1,0:T(8,128)(2,1)S(1)}, bf16[4096,512]{1,0:T(8,128)(2,1)}, u32[]{:S(2)}) copy-start(bf16[4096,512]{1,0:T(8,128)(2,1)} %param.7) | copy-start | bytes 12582916
  0.0 3.3 %copy-start.2 = (bf16[128,512]{1,0:T(8,128)(2,1)S(1)}, bf16[128,512]{1,0:T(8,128)(2,1)}, u32[]{:S(2)}) copy-start(bf16[128,512]{1,0:T(8,128)(2,1)} %taps_ref) | copy-start | bytes 393220
  0.1 3.3 %copy-start.3 = (bf16[128,512]{1,0:T(8,128)(2,1)S(1)}, bf16[128,512]{1,0:T(8,128)(2,1)}, u32[]{:S(2)}) copy-start(bf16[128,512]{1,0:T(8,128)(2,1)} %gate_ref) | copy-start | bytes 393220
  0.1 19.5 %copy-start.4 = (bf16[256,128]{1,0:T(8,128)(2,1)S(1)}, bf16[256,128]{1,0:T(8,128)(2,1)}, u32[]{:S(2)}) copy-start(bf16[256,128]{1,0:T(8,128)(2,1)} %constant.2.clone.place_ref) | copy-start | bytes 196612
  19.6 12.9 %copy-start.1 = (bf16[512,4096]{1,0:T(8,128)(2,1)S(1)}, bf16[512,4096]{1,0:T(8,128)(2,1)}, u32[]{:S(2)}) copy-start(bf16[512,4096]{1,0:T(8,128)(2,1)} %weight_ref.7) | copy-start | bytes 12582916
  32.8 1.6 %collective-permute-start.1 = (bf16[128,1024]{1,0:T(8,128)(2,1)S(1)}, bf16[128,1024]{1,0:T(8,128)(2,1)S(1)}, u32[]{:S(2)}, u32[]{:S(2)}) collective-permute-start(bf16[128,1024]{1,0:T(8,128)(2,1)S(1)} %shard_map.71), channel_id=1, source_target_pairs={{0,1},{1,0},{2,3},{3,2},{4,5},{5,4},{6,7},{7,6},{8,9},{9,8},{10,11... | collective-permute-start | bytes 786440 | tf_op jit(solution)/shard_map/ppermute | solution.py:348
  33.2 3.1 %collective-permute-start = (bf16[128,1024]{1,0:T(8,128)(2,1)S(1)}, bf16[128,1024]{1,0:T(8,128)(2,1)S(1)}, u32[]{:S(2)}, u32[]{:S(2)}) collective-permute-start(bf16[128,1024]{1,0:T(8,128)(2,1)S(1)} %shard_map.69), channel_id=1, source_target_pairs={{0,1},{1,0},{2,3},{3,2},{4,5},{5,4},{6,7},{7,6},{8,9},{9,8},{10,11... | collective-permute-start | bytes 786440 | tf_op jit(solution)/shard_map/ppermute | solution.py:352
  34.4 8.4 %collective-permute-start.2 = (bf16[128,1024]{1,0:T(8,128)(2,1)S(1)}, bf16[128,1024]{1,0:T(8,128)(2,1)S(1)}, u32[]{:S(2)}, u32[]{:S(2)}) collective-permute-start(bf16[128,1024]{1,0:T(8,128)(2,1)S(1)} %shard_map.72), channel_id=1, source_target_pairs={{0,2},{1,3},{2,0},{3,1},{4,6},{5,7},{6,4},{7,5},{8,10},{9,11},{10,... | collective-permute-start | bytes 786440 | tf_op jit(solution)/shard_map/ppermute | solution.py:351

commit v6 on v5

--- a/solution.py
+++ b/solution.py
@@ -129,17 +129,22 @@
     )()
 
 
-def turn_kernel(flip_ref, mirror_ref, value_ref, taps_ref, gate_ref, payload_ref, gate_t_ref):
+def turn_kernel(
+    flip_ref, mirror_ref, tokens_ref, weight_ref, taps_ref, gate_ref, payload_ref, gate_t_ref
+):
     peers, both, rows = payload_ref.shape
     part = both // 2
+    value = jnp.dot(
+        tokens_ref[...], weight_ref[...], preferred_element_type=jnp.float32
+    ).astype(jnp.bfloat16)
     flipped = jnp.dot(flip_ref[...], taps_ref[...], preferred_element_type=jnp.float32)
     flipped_t = flipped.T.astype(jnp.bfloat16)
     value_t = jnp.concatenate(
         [
             lax.dot_general(
-                mirror_ref[...], value_ref[:, at : at + rows], NT, preferred_element_type=jnp.float32
-            )
-            for at in range(0, value_ref.shape[1], rows)
+                mirror_ref[...], value[:, at : at + rows], NT, preferred_element_type=jnp.float32
+            )
+            for at in range(0, value.shape[1], rows)
         ],
         axis=0,
     ).astype(jnp.bfloat16)
@@ -149,16 +154,16 @@
     gate_t_ref[...] = gate_ref[...].astype(jnp.float32).T.astype(jnp.bfloat16)
 
 
-def turned(flip, mirror, value, filter_taps, gate_rows, peers):
-    rows, channels = value.shape
+def turned(flip, mirror, tokens, value_weight, filter_taps, gate_rows, peers):
+    rows, channels = filter_taps.shape
     return pl.pallas_call(
         turn_kernel,
         out_shape=[
             jax.ShapeDtypeStruct((peers, 2 * channels // peers, rows), jnp.bfloat16),
             jax.ShapeDtypeStruct((channels, rows), jnp.bfloat16),
         ],
-        compiler_params=pltpu.CompilerParams(vmem_limit_bytes=8 * 2**20),
-    )(flip, mirror, value, filter_taps, gate_rows)
+        compiler_params=pltpu.CompilerParams(vmem_limit_bytes=24 * 2**20),
+    )(flip, mirror, tokens, value_weight, filter_taps, gate_rows)
 
 
 def conv_kernel(payload_ref, place_ref, out_ref, value_ref, taps_ref, packed_ref):
@@ -337,10 +342,9 @@
     flip, tokens, value_weight, filter_taps, gate_rows = lax.optimization_barrier(
         (flip, tokens, value_weight, filter_taps, gate_rows)
     )
-    value = jnp.dot(tokens, value_weight, preferred_element_type=jnp.float32).astype(
-        jnp.bfloat16
-    )
-    payload, gate_t = turned(flip, mirror, value, filter_taps, gate_rows, peers)
+    payload, gate_t = turned(
+        flip, mirror, tokens, value_weight, filter_taps, gate_rows, peers
+    )
     payload = lax.all_to_all(payload, "ctx", split_axis=0, concat_axis=0, tiled=True)
     conv = convolve(payload)
     conv = lax.all_to_all(conv, "ctx", split_axis=0, concat_axis=0, tiled=True)

time: 43.8 us -> 43.7 us (level)
  matrix products: 0.77 us -> 0 us
  Pallas kernels: 3.79 us -> 4.41 us
    dot_general x1 -> x0, matrix products: 0.77 us -> none  [by_blocks(): jnp.dot(tokens, value_weight, preferred_element_type=jnp.float32)]
    pallas_call x1, Pallas kernels: 0.28 us -> 0.9 us  [turned(): pl.pallas_call(turn_kernel, out_shape=[jax.ShapeDtypeStruct((peers, 2 * c...]
where the time goes in v6:
time: 43.7 us; the launch traced here: 43.5 us
  blocking collectives  26.7 us (61%)
  waiting for transfers between devices  6.77 us (15%)
  Pallas kernels  4.41 us (10%)
  local copies, waits for them, and re-layouts  2.48 us (6%)
  starting transfers between devices  2.23 us (5%)
  other arithmetic  0.8 us (2%)
    all_to_all x1, blocking collectives, by_blocks(): lax.all_to_all(payload, 'ctx', split_axis=0, concat_axis=0, tiled=True)  16 us
    all_to_all x1, blocking collectives, by_blocks(): conv = lax.all_to_all(conv, 'ctx', split_axis=0, concat_axis=0, tiled=True)  10.7 us
    ppermute x1, waiting for transfers between devices, by_blocks(): arrived = lax.ppermute(sent, 'ch', far)  6.48 us
    unnamed x12, local copies, waits for them, and re-layouts  2.48 us
    pallas_call x1, Pallas kernels, convolve(): pl.pallas_call(conv_kernel, out_shape=jax.ShapeDtypeStruct((blocks, chann...  2.08 us
    ppermute x1, starting transfers between devices, by_blocks(): arrived = lax.ppermute(sent, 'ch', far)  1.59 us
    pallas_call x4, Pallas kernels, project(): pl.pallas_call(functools.partial(project_kernel, flip), out_shape=jax.Sha...  1.31 us
    pallas_call x1, Pallas kernels, turned(): pl.pallas_call(turn_kernel, out_shape=[jax.ShapeDtypeStruct((peers, 2 * c...  0.9 us
  transfers between devices with their start and end apart: 3, of which 2 were waited for; matrix products, arithmetic and copies ran while one was open for 0% of the time, Pallas kernels for 2%

profile of v6, /device:TPU:0, one launch (start us, length us, event | category | flops | bytes accessed | tf_op | source)
XLA Modules:
  0.0 43.5 jit_solution(4859536979692408966)
XLA Ops:
  0.0 0.0 copy-start.2
  0.0 0.0 copy-start.1
  0.0 0.0 copy-start.4
  0.0 0.0 copy-start.3
  0.0 0.0 copy-start.5
  0.1 1.2 %copy-done.2 = bf16[128,4096]{1,0:T(8,128)(2,1)S(1)} copy-done((bf16[128,4096]{1,0:T(8,128)(2,1)S(1)}, bf16[128,4096]{1,0:T(8,128)(2,1)}, u32[]{:S(2)}) %copy-start.2) | copy-done | bytes 1048600
  1.2 1.3 %copy-done.1 = bf16[4096,512]{1,0:T(8,128)(2,1)S(1)} copy-done((bf16[4096,512]{1,0:T(8,128)(2,1)S(1)}, bf16[4096,512]{1,0:T(8,128)(2,1)}, u32[]{:S(2)}) %copy-start.1) | copy-done | bytes 4194328
  2.5 0.0 copy-done.4
  2.5 0.0 copy-done.3
  2.5 0.9 %shard_map.65 = (bf16[8,128,128]{2,1,0:T(8,128)(2,1)S(1)}, bf16[512,128]{1,0:T(8,128)(2,1)S(1)}) custom-call(bf16[128,128]{1,0:T(8,128)(2,1)S(1)} %get-tuple-element.15.flip_ref, bf16[128,128]{1,0:T(8,128)(2,1)S(1)} %get-tuple-element.16.mirror_ref, bf16[128,4096]{1,0:T(8,128)(2,1)S(1)} %copy-done.2, bf16[4096,512]{1,0:T(8,128)(2,1)S(1)} %copy-done.1, ...), custom_call_target="tpu_custom_call" | custom-call | tf_op jit(solution)/shard_map/pallas_call | solution.py:159
  3.4 16.0 %all_to_all.10.payload_ref = bf16[8,128,128]{2,1,0:T(8,128)(2,1)S(1)} all-to-all(bf16[8,128,128]{2,1,0:T(8,128)(2,1)S(1)} %get-tuple-element.21), channel_id=1, replica_groups=mesh['ctx'=8,'ch'=4] {'ctx'}, dimensions={0} | all-to-all | bytes 524288 | tf_op jit(solution)/shard_map/all_to_all | solution.py:348
  19.4 0.0 copy-done.5
  19.4 0.0 copy-start
  19.4 2.1 %shard_map.66 = bf16[8,64,128]{2,1,0:T(8,128)(2,1)S(1)} custom-call(bf16[8,128,128]{2,1,0:T(8,128)(2,1)S(1)} %all_to_all.10.payload_ref, bf16[256,128]{1,0:T(8,128)(2,1)S(1)} %copy-done.5), custom_call_target="tpu_custom_call" | custom-call | flops 2147483648 | bytes 393216 | tf_op jit(solution)/shard_map/pallas_call | solution.py:267
  21.5 10.7 %all_to_all.11 = bf16[8,64,128]{2,1,0:T(8,128)(2,1)S(1)} all-to-all(bf16[8,64,128]{2,1,0:T(8,128)(2,1)S(1)} %shard_map.66), channel_id=1, replica_groups=mesh['ctx'=8,'ch'=4] {'ctx'}, dimensions={0} | all-to-all | bytes 262144 | tf_op jit(solution)/shard_map/all_to_all | solution.py:350
  32.2 0.0 copy-done
  32.3 0.3 shard_map.71
  32.6 0.1 collective-permute-start.1
  32.7 0.3 shard_map.69
  33.0 0.6 %collective-permute-start = (bf16[128,1024]{1,0:T(8,128)(2,1)S(1)}, bf16[128,1024]{1,0:T(8,128)(2,1)S(1)}, u32[]{:S(2)}, u32[]{:S(2)}) collective-permute-start(bf16[128,1024]{1,0:T(8,128)(2,1)S(1)} %shard_map.69), channel_id=1, source_target_pairs={{0,1},{1,0},{2,3},{3,2},{4,5},{5,4},{6,7},{7,6},{8,9},{9,8},{10,11... | collective-permute-start | bytes 786440 | tf_op jit(solution)/shard_map/ppermute | solution.py:356
  33.6 0.3 shard_map.70.first_ref
  33.9 0.3 collective-permute-done.1.second_ref
  34.2 1.6 %collective-permute-start.2 = (bf16[128,1024]{1,0:T(8,128)(2,1)S(1)}, bf16[128,1024]{1,0:T(8,128)(2,1)S(1)}, u32[]{:S(2)}, u32[]{:S(2)}) collective-permute-start(bf16[128,1024]{1,0:T(8,128)(2,1)S(1)} %shard_map.72), channel_id=1, source_target_pairs={{0,2},{1,3},{2,0},{3,1},{4,6},{5,7},{6,4},{7,5},{8,10},{9,11},{10,... | collective-permute-start | bytes 786440 | tf_op jit(solution)/shard_map/ppermute | solution.py:355
  35.8 0.3 shard_map.68
  36.2 0.0 collective-permute-done
  36.2 6.5 %collective-permute-done.2 = bf16[128,1024]{1,0:T(8,128)(2,1)S(1)} collective-permute-done((bf16[128,1024]{1,0:T(8,128)(2,1)S(1)}, bf16[128,1024]{1,0:T(8,128)(2,1)S(1)}, u32[]{:S(2)}, u32[]{:S(2)}) %collective-permute-start.2) | collective-permute-done | bytes 262176 | tf_op jit(solution)/shard_map/ppermute | solution.py:355
  42.7 0.8 %add_convert_fusion = bf16[128,1024]{1,0:T(8,128)(2,1)} fusion(bf16[128,1024]{1,0:T(8,128)(2,1)S(1)} %collective-permute-done.2, f32[128,1024]{1,0:T(8,128)S(1)} %shard_map.68, bf16[128,1024]{1,0:T(8,128)(2,1)S(1)} %collective-permute-done), kind=kLoop, calls=%fused_computation | loop fusion | flops 655360 | bytes 1310720 | tf_op jit(solution)/shard_map/convert_element_type | solution.py:360
  (3 shorter events, 0.1 us)
Async XLA Ops:
  0.0 1.2 %copy-start.2 = (bf16[128,4096]{1,0:T(8,128)(2,1)S(1)}, bf16[128,4096]{1,0:T(8,128)(2,1)}, u32[]{:S(2)}) copy-start(bf16[128,4096]{1,0:T(8,128)(2,1)} %tokens_ref) | copy-start | bytes 3145732
  0.0 2.5 %copy-start.1 = (bf16[4096,512]{1,0:T(8,128)(2,1)S(1)}, bf16[4096,512]{1,0:T(8,128)(2,1)}, u32[]{:S(2)}) copy-start(bf16[4096,512]{1,0:T(8,128)(2,1)} %weight_ref.4) | copy-start | bytes 12582916
  0.0 2.5 %copy-start.4 = (bf16[128,512]{1,0:T(8,128)(2,1)S(1)}, bf16[128,512]{1,0:T(8,128)(2,1)}, u32[]{:S(2)}) copy-start(bf16[128,512]{1,0:T(8,128)(2,1)} %gate_ref) | copy-start | bytes 393220
  0.0 2.5 %copy-start.3 = (bf16[128,512]{1,0:T(8,128)(2,1)S(1)}, bf16[128,512]{1,0:T(8,128)(2,1)}, u32[]{:S(2)}) copy-start(bf16[128,512]{1,0:T(8,128)(2,1)} %taps_ref) | copy-start | bytes 393220
  0.0 19.4 %copy-start.5 = (bf16[256,128]{1,0:T(8,128)(2,1)S(1)}, bf16[256,128]{1,0:T(8,128)(2,1)}, u32[]{:S(2)}) copy-start(bf16[256,128]{1,0:T(8,128)(2,1)} %constant.2.clone.place_ref) | copy-start | bytes 196612
  19.4 12.8 %copy-start = (bf16[512,4096]{1,0:T(8,128)(2,1)S(1)}, bf16[512,4096]{1,0:T(8,128)(2,1)}, u32[]{:S(2)}) copy-start(bf16[512,4096]{1,0:T(8,128)(2,1)} %weight_ref.8) | copy-start | bytes 12582916
  32.6 1.6 %collective-permute-start.1 = (bf16[128,1024]{1,0:T(8,128)(2,1)S(1)}, bf16[128,1024]{1,0:T(8,128)(2,1)S(1)}, u32[]{:S(2)}, u32[]{:S(2)}) collective-permute-start(bf16[128,1024]{1,0:T(8,128)(2,1)S(1)} %shard_map.71), channel_id=1, source_target_pairs={{0,1},{1,0},{2,3},{3,2},{4,5},{5,4},{6,7},{7,6},{8,9},{9,8},{10,11... | collective-permute-start | bytes 786440 | tf_op jit(solution)/shard_map/ppermute | solution.py:352
  33.0 3.2 %collective-permute-start = (bf16[128,1024]{1,0:T(8,128)(2,1)S(1)}, bf16[128,1024]{1,0:T(8,128)(2,1)S(1)}, u32[]{:S(2)}, u32[]{:S(2)}) collective-permute-start(bf16[128,1024]{1,0:T(8,128)(2,1)S(1)} %shard_map.69), channel_id=1, source_target_pairs={{0,1},{1,0},{2,3},{3,2},{4,5},{5,4},{6,7},{7,6},{8,9},{9,8},{10,11... | collective-permute-start | bytes 786440 | tf_op jit(solution)/shard_map/ppermute | solution.py:356
  34.2 8.4 %collective-permute-start.2 = (bf16[128,1024]{1,0:T(8,128)(2,1)S(1)}, bf16[128,1024]{1,0:T(8,128)(2,1)S(1)}, u32[]{:S(2)}, u32[]{:S(2)}) collective-permute-start(bf16[128,1024]{1,0:T(8,128)(2,1)S(1)} %shard_map.72), channel_id=1, source_target_pairs={{0,2},{1,3},{2,0},{3,1},{4,6},{5,7},{6,4},{7,5},{8,10},{9,11},{10,... | collective-permute-start | bytes 786440 | tf_op jit(solution)/shard_map/ppermute | solution.py:355

commit v7 on v6

--- a/solution.py
+++ b/solution.py
@@ -281,18 +281,22 @@
     )(payload, placement(lanes))
 
 
-def gate_kernel(conv_ref, gate_ref, out_ref):
-    out_ref[...] = (
+def gate_kernel(conv_ref, gate_ref, weight_ref, own_ref, out_ref):
+    own_ref[...] = (
         conv_ref[...].astype(jnp.float32) * gate_ref[...].astype(jnp.float32)
-    ).astype(out_ref.dtype)
-
-
-def gated(conv_t, gate_t):
+    ).astype(own_ref.dtype)
+    project_kernel(3, own_ref, weight_ref, out_ref)
+
+
+def gated(conv_t, gate_t, weight, features):
     return pl.pallas_call(
         gate_kernel,
-        out_shape=jax.ShapeDtypeStruct(conv_t.shape, jnp.bfloat16),
-        compiler_params=pltpu.CompilerParams(vmem_limit_bytes=4 * 2**20),
-    )(conv_t, gate_t)
+        out_shape=[
+            jax.ShapeDtypeStruct(conv_t.shape, jnp.bfloat16),
+            jax.ShapeDtypeStruct((conv_t.shape[1], features), jnp.bfloat16),
+        ],
+        compiler_params=pltpu.CompilerParams(vmem_limit_bytes=24 * 2**20),
+    )(conv_t, gate_t, weight)
 
 
 def project_kernel(flip, own_ref, weight_ref, out_ref):
@@ -348,8 +352,8 @@
     payload = lax.all_to_all(payload, "ctx", split_axis=0, concat_axis=0, tiled=True)
     conv = convolve(payload)
     conv = lax.all_to_all(conv, "ctx", split_axis=0, concat_axis=0, tiled=True)
-    own = gated(conv.reshape(gate_t.shape), gate_t)
-    far_near = lax.ppermute(project(own, out_weight, features, 3, jnp.bfloat16), "ch", near)
+    own, far_sent = gated(conv.reshape(gate_t.shape), gate_t, out_weight, features)
+    far_near = lax.ppermute(far_sent, "ch", near)
     far_own = project(own, out_weight, features, 2, jnp.float32)
     sent = added(far_own, far_near)
     arrived = lax.ppermute(sent, "ch", far)

time: 43.7 us -> 43.6 us (level)
    pallas_call x4 -> x3, Pallas kernels: 1.31 us -> 0.99 us  [project(): pl.pallas_call(functools.partial(project_kernel, flip), out_shape=jax.Sha...]
where the time goes in v7:
time: 43.6 us; the launch traced here: 43.4 us
  blocking collectives  26.7 us (61%)
  waiting for transfers between devices  6.76 us (16%)
  Pallas kernels  4.4 us (10%)
  local copies, waits for them, and re-layouts  2.48 us (6%)
  starting transfers between devices  2.23 us (5%)
  other arithmetic  0.8 us (2%)
    all_to_all x1, blocking collectives, by_blocks(): lax.all_to_all(payload, 'ctx', split_axis=0, concat_axis=0, tiled=True)  16 us
    all_to_all x1, blocking collectives, by_blocks(): conv = lax.all_to_all(conv, 'ctx', split_axis=0, concat_axis=0, tiled=True)  10.7 us
    ppermute x1, waiting for transfers between devices, by_blocks(): arrived = lax.ppermute(sent, 'ch', far)  6.47 us
    unnamed x12, local copies, waits for them, and re-layouts  2.48 us
    pallas_call x1, Pallas kernels, convolve(): pl.pallas_call(conv_kernel, out_shape=jax.ShapeDtypeStruct((blocks, chann...  2.08 us
    ppermute x1, starting transfers between devices, by_blocks(): arrived = lax.ppermute(sent, 'ch', far)  1.6 us
    pallas_call x3, Pallas kernels, project(): pl.pallas_call(functools.partial(project_kernel, flip), out_shape=jax.Sha...  0.99 us
    pallas_call x1, Pallas kernels, turned(): pl.pallas_call(turn_kernel, out_shape=[jax.ShapeDtypeStruct((peers, 2 * c...  0.9 us
  transfers between devices with their start and end apart: 3, of which 2 were waited for; matrix products, arithmetic and copies ran while one was open for 0% of the time, Pallas kernels for 2%

profile of v7, /device:TPU:0, one launch (start us, length us, event | category | flops | bytes accessed | tf_op | source)
XLA Modules:
  0.0 43.4 jit_solution(3216780917692310667)
XLA Ops:
  0.0 0.0 copy-start.2
  0.0 0.0 copy-start.1
  0.0 0.0 copy-start.4
  0.0 0.0 copy-start.3
  0.0 0.0 copy-start.5
  0.1 1.2 %copy-done.2 = bf16[128,4096]{1,0:T(8,128)(2,1)S(1)} copy-done((bf16[128,4096]{1,0:T(8,128)(2,1)S(1)}, bf16[128,4096]{1,0:T(8,128)(2,1)}, u32[]{:S(2)}) %copy-start.2) | copy-done | bytes 1048600
  1.2 1.3 %copy-done.1 = bf16[4096,512]{1,0:T(8,128)(2,1)S(1)} copy-done((bf16[4096,512]{1,0:T(8,128)(2,1)S(1)}, bf16[4096,512]{1,0:T(8,128)(2,1)}, u32[]{:S(2)}) %copy-start.1) | copy-done | bytes 4194328
  2.5 0.0 copy-done.4
  2.5 0.0 copy-done.3
  2.5 0.9 %shard_map.65 = (bf16[8,128,128]{2,1,0:T(8,128)(2,1)S(1)}, bf16[512,128]{1,0:T(8,128)(2,1)S(1)}) custom-call(bf16[128,128]{1,0:T(8,128)(2,1)S(1)} %get-tuple-element.17.flip_ref, bf16[128,128]{1,0:T(8,128)(2,1)S(1)} %get-tuple-element.18.mirror_ref, bf16[128,4096]{1,0:T(8,128)(2,1)S(1)} %copy-done.2, bf16[4096,512]{1,0:T(8,128)(2,1)S(1)} %copy-done.1, ...), custom_call_target="tpu_custom_call" | custom-call | tf_op jit(solution)/shard_map/pallas_call | solution.py:159
  3.4 16.0 %all_to_all.10.payload_ref = bf16[8,128,128]{2,1,0:T(8,128)(2,1)S(1)} all-to-all(bf16[8,128,128]{2,1,0:T(8,128)(2,1)S(1)} %get-tuple-element.23), channel_id=1, replica_groups=mesh['ctx'=8,'ch'=4] {'ctx'}, dimensions={0} | all-to-all | bytes 524288 | tf_op jit(solution)/shard_map/all_to_all | solution.py:352
  19.4 0.0 copy-done.5
  19.4 0.0 copy-start
  19.4 2.1 %shard_map.66 = bf16[8,64,128]{2,1,0:T(8,128)(2,1)S(1)} custom-call(bf16[8,128,128]{2,1,0:T(8,128)(2,1)S(1)} %all_to_all.10.payload_ref, bf16[256,128]{1,0:T(8,128)(2,1)S(1)} %copy-done.5), custom_call_target="tpu_custom_call" | custom-call | flops 2147483648 | bytes 393216 | tf_op jit(solution)/shard_map/pallas_call | solution.py:267
  21.5 10.7 %all_to_all.11 = bf16[8,64,128]{2,1,0:T(8,128)(2,1)S(1)} all-to-all(bf16[8,64,128]{2,1,0:T(8,128)(2,1)S(1)} %shard_map.66), channel_id=1, replica_groups=mesh['ctx'=8,'ch'=4] {'ctx'}, dimensions={0} | all-to-all | bytes 262144 | tf_op jit(solution)/shard_map/all_to_all | solution.py:354
  32.2 0.0 copy-done
  32.2 0.3 shard_map.67
  32.6 0.1 collective-permute-start.1
  32.6 0.3 shard_map.69
  33.0 0.6 %collective-permute-start = (bf16[128,1024]{1,0:T(8,128)(2,1)S(1)}, bf16[128,1024]{1,0:T(8,128)(2,1)S(1)}, u32[]{:S(2)}, u32[]{:S(2)}) collective-permute-start(bf16[128,1024]{1,0:T(8,128)(2,1)S(1)} %shard_map.69), channel_id=1, source_target_pairs={{0,1},{1,0},{2,3},{3,2},{4,5},{5,4},{6,7},{7,6},{8,9},{9,8},{10,11... | collective-permute-start | bytes 786440 | tf_op jit(solution)/shard_map/ppermute | solution.py:360
  33.5 0.3 shard_map.70.first_ref
  33.9 0.3 collective-permute-done.1.second_ref
  34.2 1.6 %collective-permute-start.2 = (bf16[128,1024]{1,0:T(8,128)(2,1)S(1)}, bf16[128,1024]{1,0:T(8,128)(2,1)S(1)}, u32[]{:S(2)}, u32[]{:S(2)}) collective-permute-start(bf16[128,1024]{1,0:T(8,128)(2,1)S(1)} %shard_map.71), channel_id=1, source_target_pairs={{0,2},{1,3},{2,0},{3,1},{4,6},{5,7},{6,4},{7,5},{8,10},{9,11},{10,... | collective-permute-start | bytes 786440 | tf_op jit(solution)/shard_map/ppermute | solution.py:359
  35.8 0.3 shard_map.68
  36.1 0.0 collective-permute-done
  36.2 6.5 %collective-permute-done.2 = bf16[128,1024]{1,0:T(8,128)(2,1)S(1)} collective-permute-done((bf16[128,1024]{1,0:T(8,128)(2,1)S(1)}, bf16[128,1024]{1,0:T(8,128)(2,1)S(1)}, u32[]{:S(2)}, u32[]{:S(2)}) %collective-permute-start.2) | collective-permute-done | bytes 262176 | tf_op jit(solution)/shard_map/ppermute | solution.py:359
  42.6 0.8 %add_convert_fusion = bf16[128,1024]{1,0:T(8,128)(2,1)} fusion(bf16[128,1024]{1,0:T(8,128)(2,1)S(1)} %collective-permute-done.2, f32[128,1024]{1,0:T(8,128)S(1)} %shard_map.68, bf16[128,1024]{1,0:T(8,128)(2,1)S(1)} %collective-permute-done), kind=kLoop, calls=%fused_computation | loop fusion | flops 655360 | bytes 1310720 | tf_op jit(solution)/shard_map/convert_element_type | solution.py:364
  (2 shorter events, 0.1 us)
Async XLA Ops:
  0.0 1.2 %copy-start.2 = (bf16[128,4096]{1,0:T(8,128)(2,1)S(1)}, bf16[128,4096]{1,0:T(8,128)(2,1)}, u32[]{:S(2)}) copy-start(bf16[128,4096]{1,0:T(8,128)(2,1)} %tokens_ref) | copy-start | bytes 3145732
  0.0 2.5 %copy-start.1 = (bf16[4096,512]{1,0:T(8,128)(2,1)S(1)}, bf16[4096,512]{1,0:T(8,128)(2,1)}, u32[]{:S(2)}) copy-start(bf16[4096,512]{1,0:T(8,128)(2,1)} %weight_ref.4) | copy-start | bytes 12582916
  0.0 2.5 %copy-start.4 = (bf16[128,512]{1,0:T(8,128)(2,1)S(1)}, bf16[128,512]{1,0:T(8,128)(2,1)}, u32[]{:S(2)}) copy-start(bf16[128,512]{1,0:T(8,128)(2,1)} %gate_ref) | copy-start | bytes 393220
  0.0 2.5 %copy-start.3 = (bf16[128,512]{1,0:T(8,128)(2,1)S(1)}, bf16[128,512]{1,0:T(8,128)(2,1)}, u32[]{:S(2)}) copy-start(bf16[128,512]{1,0:T(8,128)(2,1)} %taps_ref) | copy-start | bytes 393220
  0.0 19.4 %copy-start.5 = (bf16[256,128]{1,0:T(8,128)(2,1)S(1)}, bf16[256,128]{1,0:T(8,128)(2,1)}, u32[]{:S(2)}) copy-start(bf16[256,128]{1,0:T(8,128)(2,1)} %constant.2.clone.place_ref) | copy-start | bytes 196612
  19.4 12.8 %copy-start = (bf16[512,4096]{1,0:T(8,128)(2,1)S(1)}, bf16[512,4096]{1,0:T(8,128)(2,1)}, u32[]{:S(2)}) copy-start(bf16[512,4096]{1,0:T(8,128)(2,1)} %weight_ref.8) | copy-start | bytes 12582916
  32.6 1.6 %collective-permute-start.1 = (bf16[128,1024]{1,0:T(8,128)(2,1)S(1)}, bf16[128,1024]{1,0:T(8,128)(2,1)S(1)}, u32[]{:S(2)}, u32[]{:S(2)}) collective-permute-start(bf16[128,1024]{1,0:T(8,128)(2,1)S(1)} %get-tuple-element.26), channel_id=1, source_target_pairs={{0,1},{1,0},{2,3},{3,2},{4,5},{5,4},{6,7},{7,6},{8,9},{9,8},{10,11... | collective-permute-start | bytes 786440 | tf_op jit(solution)/shard_map/ppermute | solution.py:356
  33.0 3.2 %collective-permute-start = (bf16[128,1024]{1,0:T(8,128)(2,1)S(1)}, bf16[128,1024]{1,0:T(8,128)(2,1)S(1)}, u32[]{:S(2)}, u32[]{:S(2)}) collective-permute-start(bf16[128,1024]{1,0:T(8,128)(2,1)S(1)} %shard_map.69), channel_id=1, source_target_pairs={{0,1},{1,0},{2,3},{3,2},{4,5},{5,4},{6,7},{7,6},{8,9},{9,8},{10,11... | collective-permute-start | bytes 786440 | tf_op jit(solution)/shard_map/ppermute | solution.py:360
  34.2 8.4 %collective-permute-start.2 = (bf16[128,1024]{1,0:T(8,128)(2,1)S(1)}, bf16[128,1024]{1,0:T(8,128)(2,1)S(1)}, u32[]{:S(2)}, u32[]{:S(2)}) collective-permute-start(bf16[128,1024]{1,0:T(8,128)(2,1)S(1)} %shard_map.71), channel_id=1, source_target_pairs={{0,2},{1,3},{2,0},{3,1},{4,6},{5,7},{6,4},{7,5},{8,10},{9,11},{10,... | collective-permute-start | bytes 786440 | tf_op jit(solution)/shard_map/ppermute | solution.py:359
